TPU v7x, 32 devices: a whole 2x2x4 slice. The times are simulated.
32 devices in a mesh: shard: 2 (over y), ctx: 4 (over z), tp: 4 (over x, core).
Axes of the slice: x: 2, y: 2, z: 4, core: 2. Of those that a mesh axis runs over, the one named last changes fastest.
Arguments:
- prompt_x: bfloat16 [4, 1024, 1024], P('shard', 'ctx'), may hold values from -6 to 6
- cont_x: bfloat16 [32, 128, 1024], P(('shard', 'ctx')), may hold values from -6 to 6
- owner: int32 [32], P(('shard', 'ctx')), may hold values from 0 to 3, as said below
- w_query: bfloat16 [1024, 1024], P('shard', 'tp'), may hold values from -0.1875 to 0.1875
- w_key: bfloat16 [1024, 1024], P('shard', 'tp'), may hold values from -0.1875 to 0.1875
- w_value: bfloat16 [1024, 1024], P('shard', 'tp'), may hold values from -0.1875 to 0.1875
- w_out: bfloat16 [1024, 1024], P('tp', 'shard'), may hold values from -0.1875 to 0.1875
- w_up: bfloat16 [1024, 4096], P('shard', 'tp'), may hold values from -0.1875 to 0.1875
- w_down: bfloat16 [4096, 1024], P('tp', 'shard'), may hold values from -0.09375 to 0.09375
- ln_gain: bfloat16 [4, 1024], P(None, 'shard'), may hold values from 0.099609375 to 1.8984375
- ln_bias: bfloat16 [4, 1024], P(None, 'shard'), may hold values from -3 to 3
- prompt_grad: bfloat16 [4, 1024, 1024], P('shard', 'ctx'), may hold values from -6 to 6
- cont_grad: bfloat16 [32, 128, 1024], P(('shard', 'ctx')), may hold values from -6 to 6
Outputs:
- prompt_out: bfloat16 [4, 1024, 1024], P('shard', 'ctx')
- cont_out: bfloat16 [32, 128, 1024], P(('shard', 'ctx'))
- prompt_dx: bfloat16 [4, 1024, 1024], P('shard', 'ctx')
- cont_dx: bfloat16 [32, 128, 1024], P(('shard', 'ctx'))
- grad_query: float32 [1024, 1024], P('shard', 'tp')
- grad_key: float32 [1024, 1024], P('shard', 'tp')
- grad_value: float32 [1024, 1024], P('shard', 'tp')
- grad_out: float32 [1024, 1024], P('tp', 'shard')
- grad_up: float32 [1024, 4096], P('shard', 'tp')
- grad_down: float32 [4096, 1024], P('tp', 'shard')
- grad_gain: float32 [4, 1024], P(None, 'shard')
- grad_bias: float32 [4, 1024], P(None, 'shard')
Inputs may be any that keep to these rules, and one draw needn't show every extreme that they name: owner[n] lies on continuation n's index of shard: owner[n] // 2 == n // 16; every group is named by exactly 8 continuations.
All inputs are finite; a program needn't handle non-finite values.
Results may differ from a plain program's by a relative error of at most 0.018.
Values may be sent and summed in bfloat16 or wider, within the bound.
No kernel may reach another device: no remote copies, remote signals or barrier semaphores. Data moves between devices by JAX's collectives and lax.ppermute only.
A program may use at most 192 MiB of HBM per device.

v0:
```python
import jax
import jax.numpy as jnp
from jax import lax
from jax.sharding import PartitionSpec as P

HEAD_DIM = 64


EPSILON = 1e-05
ROPE_BASE = 10000.0
GELU_COEF = 0.7978845608028654
MASKED = -1e30


def layer_norm(inputs, norm_gain, norm_bias):
    centre = jnp.mean(inputs, axis=-1, keepdims=True)
    centred = inputs - centre
    spread = jnp.mean(centred * centred, axis=-1, keepdims=True)
    return centred * lax.rsqrt(spread + EPSILON) * norm_gain + norm_bias


def gelu_tanh(inputs):
    return (
        0.5 * inputs * (1.0 + jnp.tanh(GELU_COEF * (inputs + 0.044715 * inputs * inputs * inputs)))
    )


def angles(positions, head_width):
    freqs = ROPE_BASE ** (-jnp.arange(head_width // 2, dtype=jnp.float32) * (2.0 / head_width))
    theta = positions.astype(jnp.float32)[:, None] * freqs[None, :]
    return (jnp.cos(theta)[:, None, :], jnp.sin(theta)[:, None, :])


def rotate(table, cosine, sine):
    half_width = table.shape[-1] // 2
    first_half = table[..., :half_width]
    second_half = table[..., half_width:]
    return jnp.concatenate(
        [first_half * cosine - second_half * sine, first_half * sine + second_half * cosine], -1
    )


def matmul(left, right):
    return jnp.dot(left, right, preferred_element_type=jnp.float32)


def matmul_tn(left, right):
    return lax.dot_general(
        left, right, (((0,), (0,)), ((), ())), preferred_element_type=jnp.float32
    )


def matmul_nt(left, right):
    return lax.dot_general(
        left, right, (((1,), (1,)), ((), ())), preferred_element_type=jnp.float32
    )


def over_heads(partial_sum):
    return lax.psum(partial_sum, "tp")


def reduce_rows(partial_sum):
    return over_heads(partial_sum)


def scores_of(query, key_rows, allowed, scale):
    scores = (
        jnp.einsum("bqhd,bkhd->bhqk", query, key_rows, preferred_element_type=jnp.float32) * scale
    )
    return jnp.where(allowed, scores, MASKED)


def attend(query, key_rows, val_rows, allowed, scale):
    scores = scores_of(query, key_rows, allowed, scale)
    top_score = jnp.max(scores, axis=-1, keepdims=True)
    weights = jnp.exp(scores - top_score)
    totals = jnp.sum(weights, axis=-1, keepdims=True)
    probs = weights / totals
    mixed = jnp.einsum(
        "bhqk,bkhd->bqhd", probs.astype(jnp.bfloat16), val_rows, preferred_element_type=jnp.float32
    )
    return (mixed, top_score + jnp.log(totals))


def attend_back(query, key_rows, val_rows, allowed, scale, log_total, grad_mixed):
    probs = jnp.exp(scores_of(query, key_rows, allowed, scale) - log_total)
    grad_probs = jnp.einsum(
        "bqhd,bkhd->bhqk", grad_mixed, val_rows, preferred_element_type=jnp.float32
    )
    centre = jnp.sum(probs * grad_probs, axis=-1, keepdims=True)
    grad_scores = (probs * (grad_probs - centre)).astype(jnp.bfloat16)
    grad_query = (
        jnp.einsum("bhqk,bkhd->bqhd", grad_scores, key_rows, preferred_element_type=jnp.float32)
        * scale
    )
    grad_keys = (
        jnp.einsum("bhqk,bqhd->bkhd", grad_scores, query, preferred_element_type=jnp.float32)
        * scale
    )
    grad_values = jnp.einsum(
        "bhqk,bqhd->bkhd",
        probs.astype(jnp.bfloat16),
        grad_mixed,
        preferred_element_type=jnp.float32,
    )
    return (grad_query, grad_keys, grad_values)


def per_device(
    prompt_x,
    cont_x,
    owner,
    w_query,
    w_key,
    w_value,
    w_out,
    w_up,
    w_down,
    ln_gain,
    ln_bias,
    prompt_grad,
    cont_grad,
):
    full_query, full_key, full_value, full_out, full_up, full_down, gain_rows, bias_rows = (
        lax.all_gather(w_query, "shard", axis=0, tiled=True),
        lax.all_gather(w_key, "shard", axis=0, tiled=True),
        lax.all_gather(w_value, "shard", axis=0, tiled=True),
        lax.all_gather(w_out, "shard", axis=1, tiled=True),
        lax.all_gather(w_up, "shard", axis=0, tiled=True),
        lax.all_gather(w_down, "shard", axis=1, tiled=True),
        lax.all_gather(ln_gain, "shard", axis=1, tiled=True),
        lax.all_gather(ln_bias, "shard", axis=1, tiled=True),
    )
    gain_rows = gain_rows.astype(jnp.float32)
    bias_rows = bias_rows.astype(jnp.float32)
    groups = prompt_x.shape[0]
    block = prompt_x.shape[1]
    width = prompt_x.shape[2]
    conts = cont_x.shape[0]
    cont_len = cont_x.shape[1]
    prompt_len = block * lax.axis_size("ctx")
    local_width = full_query.shape[1]
    head_width = HEAD_DIM
    local_heads = local_width // head_width
    scale = head_width ** (-0.5)
    split = groups * block
    cont_rows = conts * cont_len
    all_rows = jnp.concatenate(
        [prompt_x.reshape(split, width), cont_x.reshape(cont_rows, width)], 0
    ).astype(jnp.float32)
    offset = lax.axis_index("ctx") * block
    positions = jnp.concatenate(
        [
            jnp.tile(offset + jnp.arange(block, dtype=jnp.int32), groups),
            jnp.tile(prompt_len + jnp.arange(cont_len, dtype=jnp.int32), conts),
        ]
    )
    cosine, sine = angles(positions, head_width)

    def turn(table, sign):
        return rotate(table.reshape(-1, local_heads, head_width), cosine, sign * sine).reshape(
            -1, local_width
        )

    def heads_of(table):
        return table.reshape(table.shape[0], table.shape[1], local_heads, head_width)

    normed_one = layer_norm(all_rows, gain_rows[0], bias_rows[0]).astype(jnp.bfloat16)
    query_rows = turn(matmul(normed_one, full_query), 1.0).astype(jnp.bfloat16)
    key_rows = turn(matmul(normed_one, full_key), 1.0).astype(jnp.bfloat16)
    val_rows = matmul(normed_one, full_value).astype(jnp.bfloat16)
    prompt_keys, prompt_vals = (
        lax.all_gather(
            key_rows[:split].reshape(groups, block, local_width), "ctx", axis=1, tiled=True
        ),
        lax.all_gather(
            val_rows[:split].reshape(groups, block, local_width), "ctx", axis=1, tiled=True
        ),
    )
    which = owner - lax.axis_index("shard") * groups
    picker = (which[:, None] == jnp.arange(groups, dtype=jnp.int32)[None, :]).astype(jnp.float32)
    cont_keys = jnp.concatenate(
        [prompt_keys[which], key_rows[split:].reshape(conts, cont_len, local_width)], 1
    )
    cont_vals = jnp.concatenate(
        [prompt_vals[which], val_rows[split:].reshape(conts, cont_len, local_width)], 1
    )
    query_prompt = heads_of(query_rows[:split].reshape(groups, block, local_width))
    query_cont = heads_of(query_rows[split:].reshape(conts, cont_len, local_width))
    causal = (jnp.arange(prompt_len)[None, :] <= offset + jnp.arange(block)[:, None])[None, None]
    columns = jnp.arange(prompt_len + cont_len)[None, :]
    seen = ((columns < prompt_len) | (columns - prompt_len <= jnp.arange(cont_len)[:, None]))[
        None, None
    ]
    mixed_prompt, lse_prompt = attend(
        query_prompt, heads_of(prompt_keys), heads_of(prompt_vals), causal, scale
    )
    mixed_cont, lse_cont = attend(query_cont, heads_of(cont_keys), heads_of(cont_vals), seen, scale)
    mixed_rows = jnp.concatenate(
        [mixed_prompt.reshape(split, local_width), mixed_cont.reshape(cont_rows, local_width)], 0
    ).astype(jnp.bfloat16)
    branch_one = reduce_rows(matmul(mixed_rows, full_out))
    resid_one = all_rows + layer_norm(branch_one, gain_rows[1], bias_rows[1])
    normed_three = layer_norm(resid_one, gain_rows[2], bias_rows[2]).astype(jnp.bfloat16)
    hidden_pre = matmul(normed_three, full_up)
    hidden_act = gelu_tanh(hidden_pre).astype(jnp.bfloat16)
    branch_two = reduce_rows(matmul(hidden_act, full_down))
    layer_out = (resid_one + layer_norm(branch_two, gain_rows[3], bias_rows[3])).astype(
        jnp.bfloat16
    )
    grad_all = jnp.concatenate(
        [prompt_grad.reshape(split, width), cont_grad.reshape(cont_rows, width)], 0
    ).astype(jnp.float32)
    unused_four, pull_four = jax.vjp(layer_norm, branch_two, gain_rows[3], bias_rows[3])
    grad_two, gain_four, bias_four = pull_four(grad_all)
    grad_two_b = grad_two.astype(jnp.bfloat16)
    grad_down_local = matmul_tn(hidden_act, grad_two_b)
    grad_act = matmul_nt(grad_two_b, full_down)
    unused_act, pull_gelu = jax.vjp(gelu_tanh, hidden_pre)
    grad_pre_b = pull_gelu(grad_act)[0].astype(jnp.bfloat16)
    grad_up_local = matmul_tn(normed_three, grad_pre_b)
    grad_normed_three = reduce_rows(matmul_nt(grad_pre_b, full_up))
    unused_three, pull_three = jax.vjp(layer_norm, resid_one, gain_rows[2], bias_rows[2])
    grad_resid_part, gain_three, bias_three = pull_three(grad_normed_three)
    grad_resid = grad_all + grad_resid_part
    unused_two, pull_two = jax.vjp(layer_norm, branch_one, gain_rows[1], bias_rows[1])
    grad_one, gain_two, bias_two = pull_two(grad_resid)
    grad_one_b = grad_one.astype(jnp.bfloat16)
    grad_out_local = matmul_tn(mixed_rows, grad_one_b)
    grad_mixed_b = matmul_nt(grad_one_b, full_out).astype(jnp.bfloat16)
    grad_q_prompt, grad_k_prompt, grad_v_prompt = attend_back(
        query_prompt,
        heads_of(prompt_keys),
        heads_of(prompt_vals),
        causal,
        scale,
        lse_prompt,
        heads_of(grad_mixed_b[:split].reshape(groups, block, local_width)),
    )
    grad_q_cont, grad_k_cont, grad_v_cont = attend_back(
        query_cont,
        heads_of(cont_keys),
        heads_of(cont_vals),
        seen,
        scale,
        lse_cont,
        heads_of(grad_mixed_b[split:].reshape(conts, cont_len, local_width)),
    )
    grad_k_cont = grad_k_cont.reshape(conts, prompt_len + cont_len, local_width)
    grad_v_cont = grad_v_cont.reshape(conts, prompt_len + cont_len, local_width)
    prompt_key_grad = grad_k_prompt.reshape(groups, prompt_len, local_width) + jnp.sum(
        picker[:, :, None, None] * grad_k_cont[:, None, :prompt_len], axis=0
    )
    prompt_val_grad = grad_v_prompt.reshape(groups, prompt_len, local_width) + jnp.sum(
        picker[:, :, None, None] * grad_v_cont[:, None, :prompt_len], axis=0
    )
    own_key_grad, own_val_grad = (
        lax.psum_scatter(prompt_key_grad, "ctx", scatter_dimension=1, tiled=True),
        lax.psum_scatter(prompt_val_grad, "ctx", scatter_dimension=1, tiled=True),
    )
    grad_key_rows = jnp.concatenate(
        [
            own_key_grad.reshape(split, local_width),
            grad_k_cont[:, prompt_len:].reshape(cont_rows, local_width),
        ],
        0,
    )
    grad_query_rows = jnp.concatenate(
        [grad_q_prompt.reshape(split, local_width), grad_q_cont.reshape(cont_rows, local_width)], 0
    )
    grad_key_b = turn(grad_key_rows, -1.0).astype(jnp.bfloat16)
    grad_query_b = turn(grad_query_rows, -1.0).astype(jnp.bfloat16)
    grad_val_b = jnp.concatenate(
        [
            own_val_grad.reshape(split, local_width),
            grad_v_cont[:, prompt_len:].reshape(cont_rows, local_width),
        ],
        0,
    ).astype(jnp.bfloat16)
    grad_query_local = matmul_tn(normed_one, grad_query_b)
    grad_key_local = matmul_tn(normed_one, grad_key_b)
    grad_value_local = matmul_tn(normed_one, grad_val_b)
    grad_normed_one = reduce_rows(
        matmul_nt(grad_query_b, full_query)
        + matmul_nt(grad_key_b, full_key)
        + matmul_nt(grad_val_b, full_value)
    )
    unused_one, pull_one = jax.vjp(layer_norm, all_rows, gain_rows[0], bias_rows[0])
    grad_input_part, gain_one, bias_one = pull_one(grad_normed_one)
    grad_input = (grad_resid + grad_input_part).astype(jnp.bfloat16)
    gain_local = jnp.stack([gain_one, gain_two, gain_three, gain_four], 0)
    bias_local = jnp.stack([bias_one, bias_two, bias_three, bias_four], 0)
    part_query, part_key, part_value, part_out, part_up, part_down, part_gain, part_bias = (
        lax.psum_scatter(
            grad_query_local.astype(jnp.bfloat16), "shard", scatter_dimension=0, tiled=True
        ).astype(jnp.float32),
        lax.psum_scatter(
            grad_key_local.astype(jnp.bfloat16), "shard", scatter_dimension=0, tiled=True
        ).astype(jnp.float32),
        lax.psum_scatter(
            grad_value_local.astype(jnp.bfloat16), "shard", scatter_dimension=0, tiled=True
        ).astype(jnp.float32),
        lax.psum_scatter(
            grad_out_local.astype(jnp.bfloat16), "shard", scatter_dimension=1, tiled=True
        ).astype(jnp.float32),
        lax.psum_scatter(
            grad_up_local.astype(jnp.bfloat16), "shard", scatter_dimension=0, tiled=True
        ).astype(jnp.float32),
        lax.psum_scatter(
            grad_down_local.astype(jnp.bfloat16), "shard", scatter_dimension=1, tiled=True
        ).astype(jnp.float32),
        lax.psum_scatter(
            gain_local.astype(jnp.bfloat16), "shard", scatter_dimension=1, tiled=True
        ).astype(jnp.float32),
        lax.psum_scatter(
            bias_local.astype(jnp.bfloat16), "shard", scatter_dimension=1, tiled=True
        ).astype(jnp.float32),
    )
    owned = (
        lax.psum(part_query.astype(jnp.bfloat16), "ctx").astype(jnp.float32),
        lax.psum(part_key.astype(jnp.bfloat16), "ctx").astype(jnp.float32),
        lax.psum(part_value.astype(jnp.bfloat16), "ctx").astype(jnp.float32),
        lax.psum(part_out.astype(jnp.bfloat16), "ctx").astype(jnp.float32),
        lax.psum(part_up.astype(jnp.bfloat16), "ctx").astype(jnp.float32),
        lax.psum(part_down.astype(jnp.bfloat16), "ctx").astype(jnp.float32),
        lax.psum(part_gain.astype(jnp.bfloat16), "ctx").astype(jnp.float32),
        lax.psum(part_bias.astype(jnp.bfloat16), "ctx").astype(jnp.float32),
    )
    return (
        layer_out[:split].reshape(groups, block, width),
        layer_out[split:].reshape(conts, cont_len, width),
        grad_input[:split].reshape(groups, block, width),
        grad_input[split:].reshape(conts, cont_len, width),
        owned[0],
        owned[1],
        owned[2],
        owned[3],
        owned[4],
        owned[5],
        owned[6],
        owned[7],
    )


def solution(mesh):
    placed = (
        P("shard", "ctx", None),
        P(("shard", "ctx"), None, None),
        P(("shard", "ctx")),
        P("shard", "tp"),
        P("shard", "tp"),
        P("shard", "tp"),
        P("tp", "shard"),
        P("shard", "tp"),
        P("tp", "shard"),
        P(None, "shard"),
        P(None, "shard"),
        P("shard", "ctx", None),
        P(("shard", "ctx"), None, None),
    )
    return jax.shard_map(
        per_device,
        mesh=mesh,
        in_specs=placed,
        out_specs=(
            P("shard", "ctx", None),
            P(("shard", "ctx"), None, None),
            P("shard", "ctx", None),
            P(("shard", "ctx"), None, None),
            P("shard", "tp"),
            P("shard", "tp"),
            P("shard", "tp"),
            P("tp", "shard"),
            P("shard", "tp"),
            P("tp", "shard"),
            P(None, "shard"),
            P(None, "shard"),
        ),
        check_vma=False,
    )
```

profile of v0, /device:TPU:0, one launch (start us, length us, event | category | flops | bytes accessed | tf_op | source)
XLA Modules:
  0.0 896.5 jit_solution(14288119899701253023)
XLA Ops:
  12.4 5.3 all_gather.30
  17.7 4.3 all_gather.31
  23.2 7.1 all_gather.32
  35.1 8.3 all_gather.34
  43.5 7.3 all_gather.35
  60.9 9.2 %all_gather.37 = bf16[256,1024]{1,0:T(8,128)(2,1)} all-gather(bf16[256,512]{1,0:T(8,128)(2,1)} %param.19), channel_id=1, replica_groups=mesh['shard'=2,'ctx'=4,'tp'=4] {'shard'}, dimensions={1}, use_global_device_ids=true | all-gather | bytes 786432 | tf_op jit(solution)/shard_map/all_gather | solution.py:129
  73.7 4.0 copy.120
  77.7 18.9 %all-gather.7.cloned.1.call-done = bf16[2,1024,256]{1,2,0:T(8,128)(2,1)} async-done(((bf16[2,256,256]{1,2,0:T(8,128)(2,1)}), bf16[2,1024,256]{1,2,0:T(8,128)(2,1)}) %all-gather.7.cloned.1.call-update) | async-done | bytes 1048592 | tf_op jit(solution)/shard_map/all_gather | solution.py:174
  99.6 3.4 copy-done
  106.7 5.4 fusion.41
  115.3 3.6 fusion.82
  131.1 82.3 %all-reduce.8.cloned.1.call-done = f32[1024,1024]{1,0:T(8,128)} async-done(((f32[1024,1024]{1,0:T(8,128)}), f32[1024,1024]{1,0:T(8,128)}) %all-reduce.8.cloned.1.call-update) | async-done | bytes 4194320 | tf_op jit(solution)/shard_map/psum | solution.py:60
  224.1 7.2 fusion.69
  231.3 7.6 fusion.67
  239.0 85.7 %all-reduce.10.cloned.1.call-done = f32[1024,1024]{1,0:T(8,128)} async-done(((f32[1024,1024]{1,0:T(8,128)}), f32[1024,1024]{1,0:T(8,128)}) %all-reduce.10.cloned.1.call-update) | async-done | bytes 4194320 | tf_op jit(solution)/shard_map/psum | solution.py:60
  333.5 4.0 fusion.73
  337.5 6.1 fusion.23
  344.9 4.4 fusion.86
  350.1 85.1 %all-reduce.12.cloned.1.call-done = f32[1024,1024]{1,0:T(8,128)} async-done(((f32[1024,1024]{1,0:T(8,128)}), f32[1024,1024]{1,0:T(8,128)}) %all-reduce.12.cloned.1.call-update) | async-done | bytes 4194320 | tf_op jit(solution)/shard_map/psum | solution.py:60
  435.2 5.4 multiply_reduce_fusion.4
  443.3 3.9 multiply_reduce_fusion.5
  452.5 7.8 fusion.12
  460.4 4.8 multiply_reduce_fusion
  465.6 4.7 slice.169
  470.4 5.4 copy.140
  475.8 7.5 multiply_convert_fusion
  490.2 5.5 copy.134
  495.7 6.0 multiply_reduce_fusion.3
  509.7 6.3 multiply_reduce_fusion.1
  517.6 6.2 fusion.29
  532.4 3.8 fusion.35
  538.6 23.2 %reduce-scatter.15.cloned.1.call-done = f32[2,256,256]{2,1,0:T(8,128)} async-done(((f32[2,1024,256]{2,1,0:T(8,128)}), f32[2,256,256]{2,1,0:T(8,128)}) %reduce-scatter.15.cloned.1.call-update) | async-done | bytes 524304 | tf_op jit(solution)/shard_map/reduce_scatter | solution.py:259
  570.5 36.8 %reduce-scatter.17.cloned.1.call-done = f32[2,256,256]{2,1,0:T(8,128)} async-done(((f32[2,1024,256]{2,1,0:T(8,128)}), f32[2,256,256]{2,1,0:T(8,128)}) %reduce-scatter.17.cloned.1.call-update) | async-done | bytes 524304 | tf_op jit(solution)/shard_map/reduce_scatter | solution.py:260
  608.3 6.2 add_add_fusion.4
  615.6 3.8 convolution_convert_fusion.2
  619.5 7.8 convolution_convert_fusion
  627.6 7.1 convolution_convert_fusion.1
  641.2 3.7 convolution_convert_fusion.4
  645.0 54.5 %all-reduce.14.cloned.1.call-done = f32[1024,1024]{1,0:T(8,128)} async-done(((f32[1024,1024]{1,0:T(8,128)}), f32[1024,1024]{1,0:T(8,128)}) %all-reduce.14.cloned.1.call-update) | async-done | bytes 4194320 | tf_op jit(solution)/shard_map/psum | solution.py:60
  699.6 3.9 fusion.70
  708.9 10.6 %reduce-scatter.23.cloned.1.call-done = bf16[512,256]{1,0:T(8,128)(2,1)} async-done(((bf16[1024,256]{1,0:T(8,128)(2,1)}), bf16[512,256]{1,0:T(8,128)(2,1)}) %reduce-scatter.23.cloned.1.call-update) | async-done | bytes 262160 | tf_op jit(solution)/shard_map/reduce_scatter | solution.py:301
  719.6 17.2 %reduce-scatter.19.cloned.1.call-done = bf16[512,256]{1,0:T(8,128)(2,1)} async-done(((bf16[1024,256]{1,0:T(8,128)(2,1)}), bf16[512,256]{1,0:T(8,128)(2,1)}) %reduce-scatter.19.cloned.1.call-update) | async-done | bytes 262160 | tf_op jit(solution)/shard_map/reduce_scatter | solution.py:295
  736.8 17.2 %reduce-scatter.21.cloned.1.call-done = bf16[512,256]{1,0:T(8,128)(2,1)} async-done(((bf16[1024,256]{1,0:T(8,128)(2,1)}), bf16[512,256]{1,0:T(8,128)(2,1)}) %reduce-scatter.21.cloned.1.call-update) | async-done | bytes 262160 | tf_op jit(solution)/shard_map/reduce_scatter | solution.py:298
  757.2 3.9 add_convert_fusion
  762.6 5.7 reduce-scatter.31.cloned.1.call-done
  769.3 12.9 %reduce-scatter.33.cloned.1.call-done = bf16[512,4]{1,0:T(8,128)(2,1)} async-done(((bf16[1024,4]{1,0:T(8,128)(2,1)}), bf16[512,4]{1,0:T(8,128)(2,1)}) %reduce-scatter.33.cloned.1.call-update) | async-done | bytes 4112
  783.3 12.8 %all-reduce = (bf16[4,512]{1,0:T(4,128)(2,1)S(1)}, bf16[4,512]{1,0:T(4,128)(2,1)S(1)}) all-reduce(bf16[4,512]{1,0:T(4,128)(2,1)S(1)} %copy.146, bf16[4,512]{1,0:T(4,128)(2,1)S(1)} %copy.148), channel_id=1, replica_groups=mesh['shard'=2,'ctx'=4,'tp'=4] {'ctx'}, use_global_device_ids=true, to_apply=%region_47.48 | all-reduce | flops 4096 | bytes 16384 | tf_op jit(solution)/shard_map/psum | solution.py:327
  797.3 80.3 %all-reduce.16.cloned.1.call-done = (bf16[512,256]{1,0:T(8,128)(2,1)}, bf16[512,256]{1,0:T(8,128)(2,1)}, bf16[512,256]{1,0:T(8,128)(2,1)}, bf16[256,512]{1,0:T(8...) async-done(((bf16[512,256]{1,0:T(8,128)(2,1)}, bf16[512,256]{1,0:T(8,128)(2,1)}, bf16[512,256]{1,0:T(8,128)(2,1)}, bf16[256,512]{1,0:T(8,128)(2,1)}, ...) | async-done | bytes 3145744 | tf_op jit(solution)/shard_map/psum | solution.py:321
  (380 shorter events, 145.0 us)
Async XLA Ops:
  8.0 22.3 %copy-start.8 = (bf16[4,128,1024]{2,1,0:T(8,128)(2,1)S(1)}, bf16[4,128,1024]{2,1,0:T(8,128)(2,1)}, u32[]{:S(2)}) copy-start(bf16[4,128,1024]{2,1,0:T(8,128)(2,1)} %param.14) | copy-start | bytes 3145732
  8.0 22.3 %copy-start.10 = (bf16[2,256,1024]{2,1,0:T(8,128)(2,1)S(1)}, bf16[2,256,1024]{2,1,0:T(8,128)(2,1)}, u32[]{:S(2)}) copy-start(bf16[2,256,1024]{2,1,0:T(8,128)(2,1)} %param.13) | copy-start | bytes 3145732
  8.0 9.7 %copy-start.80 = (bf16[4,512]{1,0:T(4,128)(2,1)S(1)}, bf16[4,512]{1,0:T(4,128)(2,1)}, u32[]{:S(2)}) copy-start(bf16[4,512]{1,0:T(4,128)(2,1)} %param.23) | copy-start | bytes 12292
  8.1 15.2 %copy-start.52 = (bf16[512,256]{1,0:T(8,128)(2,1)S(1)}, bf16[512,256]{1,0:T(8,128)(2,1)}, u32[]{:S(2)}) copy-start(bf16[512,256]{1,0:T(8,128)(2,1)} %param.18) | copy-start | bytes 786436
  8.1 62.4 %all-gather.5.cloned.1.call-start = ((), (), s32[]{:S(2)}) async-start(), calls=%async_computation.10 | async-start | bytes 1310720 | tf_op jit(solution)/shard_map/all_gather | solution.py:177
  10.2 24.0 %copy-start.56 = (f32[1024]{0:T(1024)}, f32[1024]{0:T(1024)S(1)}, u32[]{:S(2)}) copy-start(f32[1024]{0:T(1024)S(1)} %broadcast_multiply_fusion.4) | copy-start | bytes 12292
  12.4 9.6 %copy-start.66 = (f32[1024]{0:T(1024)}, f32[1024]{0:T(1024)S(1)}, u32[]{:S(2)}) copy-start(f32[1024]{0:T(1024)S(1)} %fusion.24) | copy-start | bytes 12292
  12.4 21.7 %copy-start.62 = (f32[1024]{0:T(1024)}, f32[1024]{0:T(1024)S(1)}, u32[]{:S(2)}) copy-start(f32[1024]{0:T(1024)S(1)} %fusion.55) | copy-start | bytes 12292
  23.2 10.9 %copy-start.58 = (f32[1,1024]{1,0:T(1,128)}, f32[1,1024]{1,0:T(1,128)S(1)}, u32[]{:S(2)}) copy-start(f32[1,1024]{1,0:T(1,128)S(1)} %get-tuple-element.73) | copy-start | bytes 12292
  33.4 10.0 %copy-start.54 = (bf16[512,256]{1,0:T(8,128)(2,1)S(1)}, bf16[512,256]{1,0:T(8,128)(2,1)}, u32[]{:S(2)}) copy-start(bf16[512,256]{1,0:T(8,128)(2,1)} %param.17) | copy-start | bytes 786436
  35.0 61.7 %all-gather.7.cloned.1.call-start = ((), (), s32[]{:S(2)}) async-start(), calls=%async_computation.11 | async-start | bytes 1310720 | tf_op jit(solution)/shard_map/all_gather | solution.py:174
  35.0 19.4 %copy-start.18 = (bf16[1024,1024]{1,0:T(8,128)(2,1)S(1)}, bf16[1024,1024]{1,0:T(8,128)(2,1)}, u32[]{:S(2)}) copy-start(bf16[1024,1024]{1,0:T(8,128)(2,1)} %copy-done.17) | copy-start | bytes 6291460
  43.5 11.7 %copy-start.31 = (bf16[1024,256]{1,0:T(8,128)(2,1)}, bf16[1024,256]{1,0:T(8,128)(2,1)S(1)}, u32[]{:S(2)}) copy-start(bf16[1024,256]{1,0:T(8,128)(2,1)S(1)} %all_gather.34) | copy-start | bytes 1572868
  57.2 156.2 %all-reduce.8.cloned.1.call-start = ((), (), s32[]{:S(2)}) async-start(), calls=%async_computation.12 | async-start | bytes 8388608 | tf_op jit(solution)/shard_map/psum | solution.py:60
  59.1 18.7 %copy-start.78 = (s32[1024]{0:T(1024)}, s32[1024]{0:T(1024)S(1)}, u32[]{:S(2)}) copy-start(s32[1024]{0:T(1024)S(1)} %pad_clamp_fusion) | copy-start | bytes 12292
  60.9 35.7 %copy-start.39 = (bf16[512,4,64]{0,2,1:T(8,128)(2,1)}, bf16[512,4,64]{0,2,1:T(8,128)(2,1)S(1)}, u32[]{:S(2)}) copy-start(bf16[512,4,64]{0,2,1:T(8,128)(2,1)S(1)} %get-tuple-element.63) | copy-start | bytes 786436
  129.4 94.7 %all-gather.9.cloned.1.call-start = ((), (), s32[]{:S(2)}) async-start(), calls=%async_computation.13 | async-start | bytes 3145728 | tf_op jit(solution)/shard_map/all_gather | solution.py:130
  130.0 101.3 %all-gather.11.cloned.1.call-start = ((), (), s32[]{:S(2)}) async-start(), calls=%async_computation.14 | async-start | bytes 3145728 | tf_op jit(solution)/shard_map/all_gather | solution.py:131
  130.6 88.1 %copy-start.64 = (f32[1,1024]{1,0:T(1,128)S(1)}, f32[1,1024]{1,0:T(1,128)}, u32[]{:S(2)}) copy-start(f32[1,1024]{1,0:T(1,128)} %get-tuple-element.72) | copy-start | bytes 12292
  130.6 88.1 %copy-start.73 = (f32[1,1024]{1,0:T(1,128)S(1)}, f32[1,1024]{1,0:T(1,128)}, u32[]{:S(2)}) copy-start(f32[1,1024]{1,0:T(1,128)} %get-tuple-element.76) | copy-start | bytes 12292
  130.6 194.1 %all-reduce.10.cloned.1.call-start = ((), (), s32[]{:S(2)}) async-start(), calls=%async_computation.15 | async-start | bytes 8388608 | tf_op jit(solution)/shard_map/psum | solution.py:60
  238.9 91.2 %copy-start.23 = (bf16[2,256,1024]{2,1,0:T(8,128)(2,1)S(1)}, bf16[2,256,1024]{2,1,0:T(8,128)(2,1)}, u32[]{:S(2)}) copy-start(bf16[2,256,1024]{2,1,0:T(8,128)(2,1)} %param.24) | copy-start | bytes 3145732
  238.9 91.2 %copy-start.25 = (bf16[4,128,1024]{2,1,0:T(8,128)(2,1)S(1)}, bf16[4,128,1024]{2,1,0:T(8,128)(2,1)}, u32[]{:S(2)}) copy-start(bf16[4,128,1024]{2,1,0:T(8,128)(2,1)} %param.25) | copy-start | bytes 3145732
  239.0 91.2 %copy-start.68 = (f32[1,1024]{1,0:T(1,128)S(1)}, f32[1,1024]{1,0:T(1,128)}, u32[]{:S(2)}) copy-start(f32[1,1024]{1,0:T(1,128)} %get-tuple-element.70) | copy-start | bytes 12292
  239.0 196.2 %all-reduce.12.cloned.1.call-start = ((), (), s32[]{:S(2)}) async-start(), calls=%async_computation.16 | async-start | bytes 8388608 | tf_op jit(solution)/shard_map/psum | solution.py:60
  349.4 212.3 %reduce-scatter.15.cloned.1.call-start = ((), (), s32[]{:S(2)}) async-start(), calls=%async_computation.17 | async-start | bytes 2621440 | tf_op jit(solution)/shard_map/reduce_scatter | solution.py:259
  451.1 9.2 %slice-start.2 = ((s8[9437184]{0:T(1024)(128)(4,1)}), s8[1048576]{0:T(1024)(128)(4,1)S(1)}, s32[]{:S(2)}) async-start(s8[9437184]{0:T(1024)(128)(4,1)} %bitcast.146), calls=%async_computation.31 | async-start | bytes 2097152
  517.6 89.7 %reduce-scatter.17.cloned.1.call-start = ((), (), s32[]{:S(2)}) async-start(), calls=%async_computation.18 | async-start | bytes 2621440 | tf_op jit(solution)/shard_map/reduce_scatter | solution.py:260
  529.0 170.5 %all-reduce.14.cloned.1.call-start = ((), (), s32[]{:S(2)}) async-start(), calls=%async_computation.19 | async-start | bytes 8388608 | tf_op jit(solution)/shard_map/psum | solution.py:60
  538.5 25.0 %copy-start.49 = (f32[1024,32]{0,1:T(8,128)S(1)}, f32[1024,32]{0,1:T(8,128)}, u32[]{:S(2)}) copy-start(f32[1024,32]{0,1:T(8,128)} %copy-done.48) | copy-start | bytes 393220
  567.8 40.6 %copy-start.47 = (bf16[1024,256]{1,0:T(8,128)(2,1)S(1)}, bf16[1024,256]{1,0:T(8,128)(2,1)}, u32[]{:S(2)}) copy-start(bf16[1024,256]{1,0:T(8,128)(2,1)} %copy-done.46) | copy-start | bytes 1572868
  614.6 94.3 %reduce-scatter.25.cloned.1.call-start = ((), (), s32[]{:S(2)}) async-start(), calls=%async_computation.23 | async-start | bytes 786432 | tf_op jit(solution)/shard_map/reduce_scatter | solution.py:304
  619.4 8.2 copy-start.86
  619.5 89.5 %reduce-scatter.29.cloned.1.call-start = ((), (), s32[]{:S(2)}) async-start(), calls=%async_computation.25 | async-start | bytes 3145728 | tf_op jit(solution)/shard_map/reduce_scatter | solution.py:310
  627.4 81.6 %reduce-scatter.27.cloned.1.call-start = ((), (), s32[]{:S(2)}) async-start(), calls=%async_computation.24 | async-start | bytes 3145728 | tf_op jit(solution)/shard_map/reduce_scatter | solution.py:307
  634.8 84.8 %reduce-scatter.23.cloned.1.call-start = ((), (), s32[]{:S(2)}) async-start(), calls=%async_computation.22 | async-start | bytes 786432 | tf_op jit(solution)/shard_map/reduce_scatter | solution.py:301
  636.4 100.3 %reduce-scatter.19.cloned.1.call-start = ((), (), s32[]{:S(2)}) async-start(), calls=%async_computation.20 | async-start | bytes 786432 | tf_op jit(solution)/shard_map/reduce_scatter | solution.py:295
  639.2 60.4 %copy-start.9 = (bf16[4,128,1024]{2,1,0:T(8,128)(2,1)S(1)}, bf16[4,128,1024]{2,1,0:T(8,128)(2,1)}, u32[]{:S(2)}) copy-start(bf16[4,128,1024]{2,1,0:T(8,128)(2,1)} %param.14) | copy-start | bytes 3145732
  639.2 60.4 %copy-start.11 = (bf16[2,256,1024]{2,1,0:T(8,128)(2,1)S(1)}, bf16[2,256,1024]{2,1,0:T(8,128)(2,1)}, u32[]{:S(2)}) copy-start(bf16[2,256,1024]{2,1,0:T(8,128)(2,1)} %param.13) | copy-start | bytes 3145732
  639.2 60.4 %copy-start.57 = (f32[1024]{0:T(1024)S(1)}, f32[1024]{0:T(1024)}, u32[]{:S(2)}) copy-start(f32[1024]{0:T(1024)} %copy-done.56) | copy-start | bytes 12292
  639.2 60.4 %copy-start.59 = (f32[1,1024]{1,0:T(1,128)S(1)}, f32[1,1024]{1,0:T(1,128)}, u32[]{:S(2)}) copy-start(f32[1,1024]{1,0:T(1,128)} %copy-done.58) | copy-start | bytes 12292
  639.2 114.8 %reduce-scatter.21.cloned.1.call-start = ((), (), s32[]{:S(2)}) async-start(), calls=%async_computation.21 | async-start | bytes 786432 | tf_op jit(solution)/shard_map/reduce_scatter | solution.py:298
  645.0 58.6 %copy-start.67 = (f32[1024]{0:T(1024)S(1)}, f32[1024]{0:T(1024)}, u32[]{:S(2)}) copy-start(f32[1024]{0:T(1024)} %copy-done.66) | copy-start | bytes 12292
  645.0 58.6 %copy-start.63 = (f32[1024]{0:T(1024)S(1)}, f32[1024]{0:T(1024)}, u32[]{:S(2)}) copy-start(f32[1024]{0:T(1024)} %copy-done.62) | copy-start | bytes 12292
  645.0 123.4 %reduce-scatter.31.cloned.1.call-start = ((), (), s32[]{:S(2)}) async-start(), calls=%async_computation.26 | async-start | bytes 393216
  707.8 74.5 %reduce-scatter.33.cloned.1.call-start = ((), (), s32[]{:S(2)}) async-start(), calls=%async_computation.27 | async-start | bytes 393216
  708.8 168.8 %all-reduce.16.cloned.1.call-start = ((), (), s32[]{:S(2)}) async-start(), calls=%async_computation.28 | async-start | bytes 6291456 | tf_op jit(solution)/shard_map/psum | solution.py:321
  877.6 10.0 %copy-start.50 = (bf16[1024,512]{1,0:T(8,128)(2,1)S(1)}, bf16[1024,512]{1,0:T(8,128)(2,1)}, u32[]{:S(2)}) copy-start(bf16[1024,512]{1,0:T(8,128)(2,1)} %get-tuple-element.33) | copy-start | bytes 3145732
  (71 other events, 265.7 us)
Sparse Core Ops, SparseCore 0:
  35.1 29.6 all-gather.4
  66.9 29.6 all-gather.6
  129.5 83.7 all-reduce.7
  239.1 85.6 all-reduce.9
  349.5 85.6 all-reduce.11
  517.7 44.0 reduce-scatter.14
  564.0 43.1 reduce-scatter.16
  614.7 84.7 all-reduce.13
  754.2 123.3 all-reduce.15
Sparse Core Ops, SparseCore 1:
  131.5 31.2 all-gather.8
  164.3 33.0 all-gather.10
  619.5 13.7 reduce-scatter.24
  635.7 31.8 reduce-scatter.28
  670.3 31.8 reduce-scatter.26
  705.1 14.4 reduce-scatter.22
  722.3 14.4 reduce-scatter.18
  739.5 14.4 reduce-scatter.20
  756.7 11.6 reduce-scatter.30
  770.7 11.5 reduce-scatter.32
where the time goes:
time: 903 us; the launch traced here: 897 us
  waiting for transfers between devices  532 us (59%)
  matrix products  119 us (13%)
  other arithmetic  97.1 us (11%)
  local copies, waits for them, and re-layouts  74.7 us (8%)
  blocking collectives  54.3 us (6%)
  between operations  17.1 us (2%)
    psum x4, waiting for transfers between devices, over_heads(): return lax.psum(partial_sum, 'tp')  308 us
    psum x1, waiting for transfers between devices, per_device(): lax.psum(part_query.astype(jnp.bfloat16), 'ctx').astype(jnp.float32)  80.3 us
    reduce_scatter x1, waiting for transfers between devices, per_device(): lax.psum_scatter(prompt_val_grad, 'ctx', scatter_dimension=1, tiled=True)  36.8 us
    unnamed x211, local copies, waits for them, and re-layouts  27.2 us
    dot_general x6, matrix products, matmul_tn(): lax.dot_general(left, right, (((0,), (0,)), ((), ())), preferred_element_...  26.7 us
    reduce_scatter x1, waiting for transfers between devices, per_device(): lax.psum_scatter(prompt_key_grad, 'ctx', scatter_dimension=1, tiled=True)  23.2 us
    dot_general x6, matrix products, matmul_nt(): lax.dot_general(left, right, (((1,), (1,)), ((), ())), preferred_element_...  23.1 us
    dot_general x6, matrix products, matmul(): return jnp.dot(left, right, preferred_element_type=jnp.float32)  21.5 us
  transfers between devices with their start and end apart: 19, of which 13 were waited for; matrix products, arithmetic and copies ran while one was open for 12% of the time, Pallas kernels for 0%

commit v1 on v0

v1 whole, which is shorter than its diff:
```python
import functools

import jax
import jax.numpy as jnp
import numpy as np
from jax import lax
from jax.experimental import pallas as pl
from jax.experimental.pallas import tpu as pltpu
from jax.sharding import PartitionSpec as P

F32 = jnp.float32
BF16 = jnp.bfloat16
HEAD = 64
EPSILON = 1e-05
ROPE_BASE = 10000.0
GELU_COEF = 0.7978845608028654
MASKED = -1e30
MIB = 1024 * 1024


def nn(left, right):
    return jnp.dot(left, right, preferred_element_type=F32)


def nt(left, right):
    return lax.dot_general(left, right, (((1,), (1,)), ((), ())), preferred_element_type=F32)


def tn(left, right):
    return lax.dot_general(left, right, (((0,), (0,)), ((), ())), preferred_element_type=F32)


def mean(value):
    return jnp.mean(value, axis=-1, keepdims=True)


def norm(value):
    centred = value - mean(value)
    inverse = lax.rsqrt(mean(centred * centred) + EPSILON)
    return centred * inverse, inverse


def norm_back(normed, inverse, cotangent, gain):
    scaled = cotangent * gain
    return (scaled - mean(scaled) - normed * mean(scaled * normed)) * inverse


def tiles(count, size, body):
    @pl.loop(0, count // size)
    def _(step):
        body(pl.multiple_of(step * size, size))


def at(start, size):
    return pl.ds(pl.multiple_of(start, size), size)


def turn(value, start, tables, sign):
    rows, width = value.shape
    cosine, minus, plus = (
        jnp.concatenate([table[at(start, rows), :]] * (width // 128), axis=1) for table in tables
    )
    left = pltpu.roll(value, width - HEAD // 2, 1)
    right = pltpu.roll(value, HEAD // 2, 1)
    return value * cosine + sign * (left * minus + right * plus)


def head_rows(value, head, count=1):
    which = lax.broadcasted_iota(jnp.int32, value.shape, 0) // (HEAD * count)
    return jnp.where(which == head, value, jnp.zeros_like(value))


def head_lanes(value, head):
    which = lax.broadcasted_iota(jnp.int32, value.shape, 1) // HEAD
    return jnp.where(which == head, value, jnp.zeros_like(value))


def normed_dots(n1, raw, half, weight):
    rows, width = n1.shape
    part = width // 2
    own, other = weight
    for start in range(0, rows, 256):
        raw[start : start + 256, :] = nn(n1[start : start + 256, at(half * part, part)], own[...]) + nn(
            n1[start : start + 256, at((1 - half) * part, part)], other[...]
        )


def qkv_kernel(prompt, idx, x, gain, bias, wqa, wqb, wka, wkb, wva, wvb, cos, sa, sb, n1, q, k, v, raw):
    core, half, ctx = idx[0], idx[1], idx[2]
    rows = x.shape[0]
    own = rows // 2
    for side in range(2):
        first = (core if side == 0 else 1 - core) * own

        def one(start, first=first, side=side):
            normed, _ = norm(x[at(first + start, 32), :].astype(F32))
            n1[at(side * own + start, 32), :] = (normed * gain[...] + bias[...]).astype(BF16)

        tiles(own, 32, one)
    tables = (cos, sa, sb)

    def place(start):
        if prompt:
            return ctx * own + start % own
        return cos.shape[0] - 128

    for out, weight, scale in ((k, (wka, wkb), 1.0), (q, (wqa, wqb), HEAD**-0.5)):
        normed_dots(n1, raw, half, weight)
        for start in range(0, rows, 128):
            turned = turn(raw[start : start + 128, :], place(start), tables, 1.0)
            out[start : start + 128, :] = turned.astype(BF16) * BF16(scale)
    normed_dots(n1, raw, half, (wva, wvb))
    v[...] = raw[...].astype(BF16)


def kv_kernel(block, idx, xo, xt, gain, bias, wka, wkb, wva, wvb, cos, sa, sb, k, v, n1, raw):
    half, ctx = idx[1], idx[2]
    own = xo.shape[0]
    for side, x in enumerate((xo, xt)):

        def one(start, side=side, x=x):
            normed, _ = norm(x[at(start, 32), :].astype(F32))
            n1[at(side * own + start, 32), :] = (normed * gain[...] + bias[...]).astype(BF16)

        tiles(own, 32, one)
    normed_dots(n1, raw, half, (wka, wkb))
    for start in range(0, 2 * own, 128):
        turned = turn(raw[start : start + 128, :], (ctx ^ block) * own + start % own, (cos, sa, sb), 1.0)
        k[start : start + 128, :] = turned.astype(BF16)
    normed_dots(n1, raw, half, (wva, wvb))
    v[...] = raw[...].astype(BF16)


def prompt_kernel(idx, q, k0, k1, k2, k3, v0, v1, v2, v3, o_own, o_oth, p, vt, ot):
    ctx = idx[2]
    ks, vs = (k0, k1, k2, k3), (v0, v1, v2, v3)
    own = o_own.shape[0]
    width = q.shape[1]
    key = lax.broadcasted_iota(jnp.int32, (own, own), 0)
    row = lax.broadcasted_iota(jnp.int32, (own, own), 1)
    seen = key <= row
    for side, out in enumerate((o_own, o_oth)):
        rows = slice(side * own, (side + 1) * own)
        qt = q[rows, :].T
        for j in range(4):
            vt[:, j * own : (j + 1) * own] = vs[j][rows, :].T
        for head in range(width // HEAD):
            feats = slice(head * HEAD, (head + 1) * HEAD)
            qh = head_rows(qt, head)
            scores = []
            for j in range(4):
                part = nn(ks[j][rows, :], qh)
                if j == 0:
                    part = jnp.where(seen, part, MASKED)
                else:
                    part = part + jnp.where((ctx ^ j) < ctx, 0.0, MASKED).astype(F32)
                scores.append(part)
            top = functools.reduce(jnp.maximum, [jnp.max(s, axis=0, keepdims=True) for s in scores])
            scores = [jnp.exp(s - top) for s in scores]
            total = sum(jnp.sum(s, axis=0, keepdims=True) for s in scores)
            inverse = 1.0 / total
            for j in range(4):
                p[side, head, j * own : (j + 1) * own, :] = (scores[j] * inverse).astype(BF16)
            ot[feats, :] = nn(vt[feats, :], p[side, head])
        out[...] = ot[...].T.astype(BF16)


def cont_kernel(idx, q, k, v, k0, k1, k2, k3, v0, v1, v2, v3, o_own, o_oth, p, ps, vt, vst, ot):
    ks, vs = (k0, k1, k2, k3), (v0, v1, v2, v3)
    own = o_own.shape[0]
    width = q.shape[1]
    length = 128
    key = lax.broadcasted_iota(jnp.int32, (length, 2 * length), 0)
    row = lax.broadcasted_iota(jnp.int32, (length, 2 * length), 1) % length
    seen = key <= row
    for c in range(2 * own // length):
        group = idx[3 + c]
        mine = slice(c * length, (c + 1) * length)
        theirs = at(group * own, own)
        qt = q[mine, :].T
        for j in range(4):
            vt[:, j * own : (j + 1) * own] = vs[j][theirs, :].T
        vst[...] = v[mine, :].T
        for pair in range(width // HEAD // 2):
            feats = slice(pair * 2 * HEAD, (pair + 1) * 2 * HEAD)
            q2 = jnp.concatenate([head_rows(qt, 2 * pair), head_rows(qt, 2 * pair + 1)], axis=1)
            scores = [nn(ks[j][theirs, :], q2) for j in range(4)]
            scores.append(jnp.where(seen, nn(k[mine, :], q2), MASKED))
            top = functools.reduce(jnp.maximum, [jnp.max(s, axis=0, keepdims=True) for s in scores])
            scores = [jnp.exp(s - top) for s in scores]
            total = sum(jnp.sum(s, axis=0, keepdims=True) for s in scores)
            inverse = 1.0 / total
            for j in range(4):
                p[c, pair, j * own : (j + 1) * own, :] = (scores[j] * inverse).astype(BF16)
            ps[c, pair] = (scores[4] * inverse).astype(BF16)
            both = nn(vt[feats, :], p[c, pair]) + nn(vst[feats, :], ps[c, pair])
            first = pair * 2 * HEAD
            ot[first : first + HEAD, :] = both[:HEAD, :length]
            ot[first + HEAD : first + 2 * HEAD, :] = both[HEAD:, length:]
        out = o_own if c < own // length else o_oth
        place = c * length % own
        out[place : place + length, :] = ot[...].T.astype(BF16)


def after_kernel(idx, x, o0, o1, o2, o3, w0, w1, w2, w3, gain1, bias1, gain2, bias2, z, x1, n3):
    core, half = idx[0], idx[1]
    own = z.shape[0]
    part = z.shape[1] // 2
    for side in range(2):
        cols = at((half if side == 0 else 1 - half) * part, part)
        z[:, cols] = sum(nn(o[...], w[side]) for o, w in ((o0, w0), (o1, w1), (o2, w2), (o3, w3)))

    def one(start):
        rows = at(start, 32)
        normed, _ = norm(z[rows, :])
        after = x[at(core * own + start, 32), :].astype(F32) + (normed * gain1[...] + bias1[...])
        x1[rows, :] = after
        normed, _ = norm(after)
        n3[rows, :] = (normed * gain2[...] + bias2[...]).astype(BF16)

    tiles(own, 32, one)


def up_down_kernel(idx, n3o, n3t, wua, wub, wda, wdb, act, slope, keep, send):
    half = idx[1]
    own = n3o.shape[0]
    part = n3o.shape[1] // 2
    for start in range(0, act.shape[1], 256):
        cols = slice(start, start + 256)
        for side, n3 in enumerate((n3o, n3t)):
            rows = slice(side * own, (side + 1) * own)
            pre = nn(n3[:, at(half * part, part)], wua[:, cols]) + nn(
                n3[:, at((1 - half) * part, part)], wub[:, cols]
            )
            square = pre * pre
            tanh = jnp.tanh(GELU_COEF * (pre + 0.044715 * pre * square))
            up = 0.5 * (1.0 + tanh)
            act[rows, cols] = (pre * up).astype(BF16)
            inner = GELU_COEF * (1.0 + (3.0 * 0.044715) * square)
            slope[rows, cols] = (up + 0.5 * pre * (1.0 - tanh * tanh) * inner).astype(BF16)
    for side, w in enumerate((wda, wdb)):
        cols = at((half if side == 0 else 1 - half) * part, part)
        send[:, cols] = nn(act[own:, :], w[...]).astype(BF16)
        keep[:, cols] = nn(act[:own, :], w[...])


def last_kernel(idx, mine, theirs, x1, cotangent, gain, bias, y, dm, dgain, dbias):
    own = mine.shape[0]
    core = idx[0]
    dgain[...] = jnp.zeros_like(dgain)
    dbias[...] = jnp.zeros_like(dbias)

    def one(start):
        rows = at(start, 32)
        total = mine[rows, :].astype(F32) + theirs[rows, :].astype(F32)
        normed, inverse = norm(total)
        y[rows, :] = (x1[rows, :] + (normed * gain[...] + bias[...])).astype(BF16)
        dy = cotangent[at(core * own + start, 32), :].astype(F32)
        dm[rows, :] = norm_back(normed, inverse, dy, gain[...]).astype(BF16)
        dgain[...] += jnp.sum(dy * normed, axis=0, keepdims=True)
        dbias[...] += jnp.sum(dy, axis=0, keepdims=True)

    tiles(own, 32, one)


def down_up_kernel(idx, dmo, dmt, wua, wub, wda, wdb, slope, du, keep, send):
    half = idx[1]
    own = dmo.shape[0]
    part = dmo.shape[1] // 2
    for start in range(0, slope.shape[1], 256):
        cols = slice(start, start + 256)
        for side, dm in enumerate((dmo, dmt)):
            rows = slice(side * own, (side + 1) * own)
            back = nt(dm[:, at(half * part, part)], wda[cols, :]) + nt(
                dm[:, at((1 - half) * part, part)], wdb[cols, :]
            )
            du[rows, cols] = (back * slope[rows, cols].astype(F32)).astype(BF16)
    for side, w in enumerate((wua, wub)):
        cols = at((half if side == 0 else 1 - half) * part, part)
        send[:, cols] = nt(du[own:, :], w[...]).astype(BF16)
        keep[:, cols] = nt(du[:own, :], w[...])


def middle_kernel(
    idx, mine, theirs, x1, z, cotangent, gain1, gain2, dx1, dz, dgain1, dbias1, dgain2, dbias2
):
    own = mine.shape[0]
    core = idx[0]
    for total in (dgain1, dbias1, dgain2, dbias2):
        total[...] = jnp.zeros_like(total)

    def one(start):
        rows = at(start, 32)
        back = mine[rows, :].astype(F32) + theirs[rows, :].astype(F32)
        normed, inverse = norm(x1[rows, :])
        dgain2[...] += jnp.sum(back * normed, axis=0, keepdims=True)
        dbias2[...] += jnp.sum(back, axis=0, keepdims=True)
        after = cotangent[at(core * own + start, 32), :].astype(F32) + norm_back(
            normed, inverse, back, gain2[...]
        )
        dx1[rows, :] = after
        normed, inverse = norm(z[rows, :])
        dgain1[...] += jnp.sum(after * normed, axis=0, keepdims=True)
        dbias1[...] += jnp.sum(after, axis=0, keepdims=True)
        dz[rows, :] = norm_back(normed, inverse, after, gain1[...]).astype(BF16)

    tiles(own, 32, one)


def spread_out(half, dzo, dzt, woa, wob, do):
    own = dzo.shape[0]
    part = dzo.shape[1] // 2
    for side, dz in enumerate((dzo, dzt)):
        do[side * own : (side + 1) * own, :] = (
            nt(dz[:, at(half * part, part)], woa[...]) + nt(dz[:, at((1 - half) * part, part)], wob[...])
        ).astype(BF16)


def prompt_back_kernel(*refs):
    idx, dzo, dzt, woa, wob, p, q = refs[:7]
    ks, vs = refs[7:11], refs[11:15]
    cos, sa, sb, dq = refs[15:19]
    dks, dvs = refs[19:23], refs[23:27]
    do, kt, dqt, dst = refs[27:]
    half, ctx = idx[1], idx[2]
    spread_out(half, dzo, dzt, woa, wob, do)
    own = dzo.shape[0]
    width = q.shape[1]
    heads = width // HEAD
    for side in range(2):
        rows = slice(side * own, (side + 1) * own)
        dot = do[rows, :].T
        for j in range(4):
            kt[:, j * own : (j + 1) * own] = ks[j][rows, :].T
        for head in range(heads):
            feats = slice(head * HEAD, (head + 1) * HEAD)
            doh = head_rows(dot, head)
            probs = [p[side, head, j * own : (j + 1) * own, :].astype(F32) for j in range(4)]
            terms = [probs[j] * nn(vs[j][rows, :], doh) for j in range(4)]
            centre = sum(jnp.sum(t, axis=0, keepdims=True) for t in terms)
            for j in range(4):
                dst[head, j * own : (j + 1) * own, :] = (terms[j] - probs[j] * centre).astype(BF16)
            dqt[feats, :] = nn(kt[feats, :], dst[head]) * (HEAD**-0.5)
        for j in range(4):
            keys = slice(j * own, (j + 1) * own)
            dks[j][rows, :] = sum(
                nn(dst[head, keys, :], head_lanes(q[rows, :], head)) for head in range(heads)
            )
            dvs[j][rows, :] = sum(
                nn(p[side, head, keys, :], head_lanes(do[rows, :], head)) for head in range(heads)
            )
        dqf = dqt[...].T
        for start in range(0, own, 128):
            dq[side * own + start : side * own + start + 128, :] = turn(
                dqf[start : start + 128, :], ctx * own + start, (cos, sa, sb), -1.0
            ).astype(BF16)


def cont_back_kernel(*refs):
    idx, dzo, dzt, woa, wob, p, ps, q, k, v = refs[:10]
    ks, vs = refs[10:14], refs[14:18]
    adds = refs[18:26]
    cos, sa, sb, dq, dk, dv = refs[26:32]
    outs = refs[32:40]
    do, kt, kst, dqt, dst, dsst, total = refs[40:]
    half = idx[1]
    spread_out(half, dzo, dzt, woa, wob, do)
    own = dzo.shape[0]
    width = q.shape[1]
    pairs = width // HEAD // 2
    length = 128
    tables = (cos, sa, sb)
    last = cos.shape[0] - length
    for j in range(8):
        total[j] = adds[j][...]
    for c in range(2 * own // length):
        group = idx[3 + c]
        mine = slice(c * length, (c + 1) * length)
        theirs = at(group * own, own)
        dot = do[mine, :].T
        for j in range(4):
            kt[:, j * own : (j + 1) * own] = ks[j][theirs, :].T
        kst[...] = k[mine, :].T
        for pair in range(pairs):
            feats = slice(pair * 2 * HEAD, (pair + 1) * 2 * HEAD)
            do2 = jnp.concatenate([head_rows(dot, 2 * pair), head_rows(dot, 2 * pair + 1)], axis=1)
            probs = [p[c, pair, j * own : (j + 1) * own, :].astype(F32) for j in range(4)]
            probs.append(ps[c, pair].astype(F32))
            terms = [probs[j] * nn(vs[j][theirs, :], do2) for j in range(4)]
            terms.append(probs[4] * nn(v[mine, :], do2))
            centre = sum(jnp.sum(t, axis=0, keepdims=True) for t in terms)
            for j in range(4):
                dst[pair, j * own : (j + 1) * own, :] = (terms[j] - probs[j] * centre).astype(BF16)
            dsst[pair] = (terms[4] - probs[4] * centre).astype(BF16)
            both = (nn(kt[feats, :], dst[pair]) + nn(kst[feats, :], dsst[pair])) * (HEAD**-0.5)
            first = pair * 2 * HEAD
            dqt[first : first + HEAD, :] = both[:HEAD, :length]
            dqt[first + HEAD : first + 2 * HEAD, :] = both[HEAD:, length:]
        q2 = [
            jnp.concatenate([head_lanes(q[mine, :], 2 * r), head_lanes(q[mine, :], 2 * r + 1)], axis=0)
            for r in range(pairs)
        ]
        do2 = [
            jnp.concatenate([head_lanes(do[mine, :], 2 * r), head_lanes(do[mine, :], 2 * r + 1)], axis=0)
            for r in range(pairs)
        ]
        for j in range(4):
            keys = slice(j * own, (j + 1) * own)
            total[j, theirs, :] += sum(nn(dst[r, keys, :], q2[r]) for r in range(pairs))
            total[4 + j, theirs, :] += sum(nn(p[c, r, keys, :], do2[r]) for r in range(pairs))
        dkf = sum(nn(dsst[r], q2[r]) for r in range(pairs))
        dv[mine, :] = sum(nn(ps[c, r], do2[r]) for r in range(pairs)).astype(BF16)
        dk[mine, :] = turn(dkf, last, tables, -1.0).astype(BF16)
        dq[mine, :] = turn(dqt[...].T, last, tables, -1.0).astype(BF16)
    for j in range(8):
        outs[j][...] = total[j].astype(BF16)


def input_kernel(turned, idx, dq, dk, dv, wqa, wqb, wka, wkb, wva, wvb, keep, send):
    half = idx[1]
    own = dq.shape[0] // 2
    part = keep.shape[1] // 2
    for side, weights in enumerate(((wqa, wka, wva), (wqb, wkb, wvb))):
        cols = at((half if side == 0 else 1 - half) * part, part)
        for rows, out in ((slice(own, 2 * own), send), (slice(0, own), keep)):
            total = sum(nt(d[rows, :], w[...]) for d, w in zip((dq, dk, dv), weights))
            out[:, cols] = total.astype(out.dtype)


def unturn_kernel(idx, k_own, k1, k2, v_own, v1, v2, cos, sa, sb, dk, dv):
    ctx = idx[2]
    rows = dk.shape[0]
    own = rows // 2
    for start in range(0, rows, 128):
        r = slice(start, start + 128)
        total = k_own[r, :].astype(F32) + k1[r, :].astype(F32) + k2[r, :].astype(F32)
        dk[r, :] = turn(total, ctx * own + start % own, (cos, sa, sb), -1.0).astype(BF16)
    dv[...] = (v_own[...].astype(F32) + v1[...].astype(F32) + v2[...].astype(F32)).astype(BF16)


def first_kernel(idx, mine, theirs, x, dx1, gain, dx, dgain, dbias):
    own = mine.shape[0]
    core = idx[0]
    dgain[...] = jnp.zeros_like(dgain)
    dbias[...] = jnp.zeros_like(dbias)

    def one(start):
        rows = at(start, 32)
        back = mine[rows, :].astype(F32) + theirs[rows, :].astype(F32)
        normed, inverse = norm(x[at(core * own + start, 32), :].astype(F32))
        dgain[...] += jnp.sum(back * normed, axis=0, keepdims=True)
        dbias[...] += jnp.sum(back, axis=0, keepdims=True)
        dx[rows, :] = (dx1[rows, :] + norm_back(normed, inverse, back, gain[...])).astype(BF16)

    tiles(own, 32, one)


def call(kernel, idx, inputs, outputs, scratch=(), flops=0, mib=40, name=None):
    shapes = [jax.ShapeDtypeStruct(shape, dtype) for shape, dtype in outputs]
    moved = sum(int(np.prod(a.shape)) * a.dtype.itemsize for a in [*inputs, *shapes])
    vmem = pl.BlockSpec(memory_space=pltpu.VMEM)
    return pl.pallas_call(
        kernel,
        out_shape=shapes,
        in_specs=[pl.BlockSpec(memory_space=pltpu.SMEM)] + [vmem] * len(inputs),
        out_specs=[vmem] * len(outputs),
        scratch_shapes=list(scratch),
        compiler_params=pltpu.CompilerParams(vmem_limit_bytes=mib * MIB),
        cost_estimate=pl.CostEstimate(flops=int(flops), bytes_accessed=moved, transcendentals=0),
        name=name,
    )(idx, *inputs)


def rope_tables(length):
    freqs = ROPE_BASE ** (-np.arange(HEAD // 2, dtype=np.float32) * np.float32(2.0 / HEAD))
    theta = np.arange(length, dtype=np.float32)[:, None] * freqs.astype(np.float32)[None, :]
    cosine, sine = np.cos(theta), np.sin(theta)
    none = np.zeros_like(sine)
    return tuple(
        jnp.asarray(np.tile(np.concatenate(pair, axis=1), (1, 2)).astype(np.float32))
        for pair in ((cosine, cosine), (-sine, none), (none, sine))
    )


def swap(value, axis, bit):
    size = lax.axis_size(axis)
    return lax.ppermute(value, axis, [(i, i ^ bit) for i in range(size)])


def per_device(
    prompt_x,
    cont_x,
    owner,
    w_query,
    w_key,
    w_value,
    w_out,
    w_up,
    w_down,
    ln_gain,
    ln_bias,
    prompt_grad,
    cont_grad,
):
    shards = lax.axis_size("shard")
    groups, block, width = prompt_x.shape
    conts, cont_len, _ = cont_x.shape
    local = w_query.shape[1]
    hidden = w_up.shape[1]
    rows = groups * block
    own = rows // 2
    prompt_len = block * lax.axis_size("ctx")
    core = lax.axis_index("tp") % 2
    shard = lax.axis_index("shard")
    ctx = lax.axis_index("ctx")

    def both(weight, dim):
        if shards == 2:
            return weight, swap(weight, "shard", 1)
        full = lax.all_gather(weight, "shard", axis=dim, tiled=True)
        return tuple(jnp.split(full, 2, axis=dim))

    half = shard if shards == 2 else jnp.zeros_like(shard)
    which = (owner - shard * groups).reshape(2, conts // 2)
    which = jnp.where(core == 1, which[::-1], which) ^ core
    idx = jnp.concatenate([jnp.stack([core, half, ctx]), which.reshape(conts)]).astype(jnp.int32)

    wk, wv, wq = both(w_key, 0), both(w_value, 0), both(w_query, 0)
    wo = both(w_out, 1)
    wu, wd = both(w_up, 0), both(w_down, 1)
    wo0 = jnp.stack(wo)
    wo1 = swap(wo0, "tp", 1)
    wo2 = swap(wo0, "tp", 2)
    wo3 = swap(wo2, "tp", 1)

    def wide(small):
        full = lax.all_gather(small, "shard", axis=1, tiled=True)
        return [full[r : r + 1].astype(F32) for r in range(4)]

    gains, biases = wide(ln_gain), wide(ln_bias)
    tables = rope_tables(prompt_len + cont_len)

    def mine(value):
        return lax.dynamic_slice_in_dim(value, core * own, own, 0)

    xs = (prompt_x.reshape(rows, width), cont_x.reshape(rows, width))
    dys = (prompt_grad.reshape(rows, width), cont_grad.reshape(rows, width))

    x_own = mine(xs[0])
    far_own = [None] + [swap(x_own, "ctx", j) for j in (1, 2)]
    far_own.append(swap(far_own[2], "ctx", 1))
    far_oth = [None] + [swap(far_own[j], "tp", 1) for j in (1, 2, 3)]

    wide_rows = (rows, local)
    raw = pltpu.VMEM(wide_rows, F32)
    qkv_flops = 2 * rows * width * local
    chunks = []
    for prompt in (True, False):
        chunks.append(
            call(
                functools.partial(qkv_kernel, prompt),
                idx,
                [xs[0 if prompt else 1], gains[0], biases[0], *wq, *wk, *wv, *tables],
                [((rows, width), BF16)] + [(wide_rows, BF16)] * 3,
                [raw],
                flops=3 * qkv_flops,
                name="qkv_prompt" if prompt else "qkv_cont",
            )
        )
    (n1p, qp, kp, vp), (n1c, qc, kc, vc) = chunks
    keys, values = [kp], [vp]
    for j in (1, 2, 3):
        k, v = call(
            functools.partial(kv_kernel, j),
            idx,
            [far_own[j], far_oth[j], gains[0], biases[0], *wk, *wv, *tables],
            [(wide_rows, BF16)] * 2,
            [pltpu.VMEM((rows, width), BF16), raw],
            flops=2 * qkv_flops,
            name=f"kv_{j}",
        )
        keys.append(k)
        values.append(v)

    attention_flops = 2 * rows * prompt_len * local * (local // HEAD)
    half_o = ((own, local), BF16)
    o_own_p, o_oth_p, probs_p = call(
        prompt_kernel,
        idx,
        [qp, *keys, *values],
        [half_o, half_o, ((2, local // HEAD, prompt_len, own), BF16)],
        [pltpu.VMEM((local, prompt_len), BF16), pltpu.VMEM((local, own), F32)],
        flops=2 * attention_flops,
        name="attend_prompt",
    )
    pairs = local // HEAD // 2
    o_own_c, o_oth_c, probs_c, probs_s = call(
        cont_kernel,
        idx,
        [qc, kc, vc, *keys, *values],
        [
            half_o,
            half_o,
            ((conts, pairs, prompt_len, 2 * cont_len), BF16),
            ((conts, pairs, cont_len, 2 * cont_len), BF16),
        ],
        [
            pltpu.VMEM((local, prompt_len), BF16),
            pltpu.VMEM((local, cont_len), BF16),
            pltpu.VMEM((local, cont_len), F32),
        ],
        flops=2 * attention_flops,
        name="attend_cont",
    )

    big = 2 * rows * width * hidden
    mixed = ((o_own_p, o_oth_p), (o_own_c, o_oth_c))
    stage = []
    for x, (o_own, o_oth) in zip(xs, mixed):
        z, x1, n3 = call(
            after_kernel,
            idx,
            [
                x,
                o_own,
                swap(o_oth, "tp", 1),
                swap(o_own, "tp", 2),
                swap(o_oth, "tp", 3),
                wo0,
                wo1,
                wo2,
                wo3,
                gains[1],
                biases[1],
                gains[2],
                biases[2],
            ],
            [((own, width), F32), ((own, width), F32), ((own, width), BF16)],
            flops=2 * own * width * width,
            name="after_attention",
        )
        n3t = swap(n3, "tp", 1)
        act, slope, keep, send = call(
            up_down_kernel,
            idx,
            [n3, n3t, *wu, *wd],
            [((rows, hidden), BF16), ((rows, hidden), BF16), ((own, width), F32), ((own, width), BF16)],
            flops=2 * big,
            name="up_down",
        )
        summed = (keep + swap(send, "tp", 1).astype(F32)).astype(BF16)
        stage.append((z, x1, n3, n3t, act, slope, summed, swap(summed, "tp", 2)))

    row = ((1, width), F32)
    later = []
    for (z, x1, n3, n3t, act, slope, summed, theirs), dy in zip(stage, dys):
        y, dm, dgain3, dbias3 = call(
            last_kernel,
            idx,
            [summed, theirs, x1, dy, gains[3], biases[3]],
            [((own, width), BF16), ((own, width), BF16), row, row],
            name="last_norm",
        )
        dmt = swap(dm, "tp", 1)
        du, keep, send = call(
            down_up_kernel,
            idx,
            [dm, dmt, *wu, *wd, slope],
            [((rows, hidden), BF16), ((own, width), F32), ((own, width), BF16)],
            flops=2 * big,
            name="down_up",
        )
        summed = (keep + swap(send, "tp", 1).astype(F32)).astype(BF16)
        later.append((y, dm, dmt, du, summed, swap(summed, "tp", 2), dgain3, dbias3))

    def stacked(first, second):
        return jnp.concatenate([*first, *second], axis=0)

    def joined(which_one, table):
        return stacked(*[[entry[i] for i in which_one] for entry in table])

    def weight_grad(left, right):
        return tn(left, right).astype(BF16)

    dm_all = joined((1, 2), later)
    grad_down = weight_grad(joined((4,), stage), dm_all)
    grad_up = weight_grad(joined((2, 3), stage), joined((3,), later))

    middle = []
    for (z, x1, *_), (_, _, _, _, summed, theirs, *_), dy in zip(stage, later, dys):
        dx1, dz, dgain1, dbias1, dgain2, dbias2 = call(
            middle_kernel,
            idx,
            [summed, theirs, x1, z, dy, gains[1], gains[2]],
            [((own, width), F32), ((own, width), BF16), row, row, row, row],
            name="middle_norms",
        )
        middle.append((dx1, dz, swap(dz, "tp", 1), dgain1, dbias1, dgain2, dbias2))
    grad_out = weight_grad(stacked(*mixed), joined((1, 2), middle))

    dqp, *grads = call(
        prompt_back_kernel,
        idx,
        [middle[0][1], middle[0][2], *wo, probs_p, qp, *keys, *values, *tables],
        [(wide_rows, BF16)] + [(wide_rows, F32)] * 8,
        [
            pltpu.VMEM(wide_rows, BF16),
            pltpu.VMEM((local, prompt_len), BF16),
            pltpu.VMEM((local, own), F32),
            pltpu.VMEM((local // HEAD, prompt_len, own), BF16),
        ],
        flops=4 * attention_flops,
        mib=48,
        name="attend_prompt_back",
    )
    dqc, dkc, dvc, *grads = call(
        cont_back_kernel,
        idx,
        [middle[1][1], middle[1][2], *wo, probs_c, probs_s, qc, kc, vc, *keys, *values, *grads, *tables],
        [(wide_rows, BF16)] * 11,
        [
            pltpu.VMEM(wide_rows, BF16),
            pltpu.VMEM((local, prompt_len), BF16),
            pltpu.VMEM((local, cont_len), BF16),
            pltpu.VMEM((local, cont_len), F32),
            pltpu.VMEM((pairs, prompt_len, 2 * cont_len), BF16),
            pltpu.VMEM((pairs, cont_len, 2 * cont_len), BF16),
            pltpu.VMEM((8, *wide_rows), F32),
        ],
        flops=4 * attention_flops,
        mib=48,
        name="attend_cont_back",
    )

    def to_owner(parts):
        ours, one, two, three = parts
        two = (two.astype(F32) + swap(three, "ctx", 1).astype(F32)).astype(BF16)
        return ours, swap(one, "ctx", 1), swap(two, "ctx", 2)

    dkp, dvp = call(
        unturn_kernel,
        idx,
        [*to_owner(grads[:4]), *to_owner(grads[4:]), *tables],
        [(wide_rows, BF16)] * 2,
        name="unturn",
    )

    dx = []
    firsts = []
    for x, (dx1, *_), gradient in zip(xs, middle, ((dqp, dkp, dvp), (dqc, dkc, dvc))):
        keep, send = call(
            functools.partial(input_kernel, True),
            idx,
            [*gradient, *wq, *wk, *wv],
            [((own, width), F32), ((own, width), BF16)],
            flops=3 * qkv_flops,
            name="input_back",
        )
        summed = (keep + swap(send, "tp", 1).astype(F32)).astype(BF16)
        out, dgain0, dbias0 = call(
            first_kernel,
            idx,
            [summed, swap(summed, "tp", 2), x, dx1, gains[0]],
            [((own, width), BF16), row, row],
            name="first_norm",
        )
        dx.append(out)
        firsts.append((dgain0, dbias0))
    n1 = jnp.concatenate([n1p, n1c], axis=0)
    grad_query, grad_key, grad_value = (
        weight_grad(n1, jnp.concatenate(pair, axis=0)) for pair in ((dqp, dqc), (dkp, dkc), (dvp, dvc))
    )

    def over_ctx(part):
        quarter = part.shape[0] // 4
        four = part.reshape(4, quarter, part.shape[1])
        near, far = ctx & 1, ctx & 2

        def pick(value, index):
            return lax.dynamic_index_in_dim(value, index, 0, keepdims=False)

        mine_two = jnp.stack([pick(four, ctx), pick(four, ctx ^ 2)])
        send_two = jnp.stack([pick(four, ctx ^ 1), pick(four, ctx ^ 3)])
        mine_two = mine_two.astype(F32) + swap(send_two, "ctx", 1).astype(F32)
        one = (mine_two[0] + swap(mine_two[1].astype(BF16), "ctx", 2).astype(F32)).astype(BF16)
        two = jnp.stack([one, swap(one, "ctx", 2)])
        other = swap(two, "ctx", 1)
        blocks = jnp.concatenate([two, other], axis=0)
        result = jnp.stack([pick(blocks, jnp.array([0, 2, 1, 3])[ctx ^ i]) for i in range(4)])
        return result.reshape(part.shape).astype(F32)

    def reduced(grad, dim):
        if shards == 2:
            size = grad.shape[dim] // 2
            ours = lax.dynamic_slice_in_dim(grad, shard * size, size, dim)
            theirs = lax.dynamic_slice_in_dim(grad, (1 - shard) * size, size, dim)
            part = (ours.astype(F32) + swap(theirs, "shard", 1).astype(F32)).astype(BF16)
        else:
            part = lax.psum_scatter(grad, "shard", scatter_dimension=dim, tiled=True)
        return over_ctx(part)

    small = [None] * 8
    for first, (_, _, _, dgain1, dbias1, dgain2, dbias2), (*_, dgain3, dbias3) in zip(firsts, middle, later):
        for place, term in zip(
            range(8), (first[0], dgain1, dgain2, dgain3, first[1], dbias1, dbias2, dbias3)
        ):
            small[place] = term if small[place] is None else small[place] + term
    small = jnp.concatenate(small, axis=0)
    small = small + swap(small, "tp", 1)
    if shards == 2:
        size = width // 2
        small = lax.dynamic_slice_in_dim(small, shard * size, size, 1) + swap(
            lax.dynamic_slice_in_dim(small, (1 - shard) * size, size, 1), "shard", 1
        )
    else:
        small = lax.psum_scatter(small, "shard", scatter_dimension=1, tiled=True)
    small = small + swap(small, "ctx", 1)
    small = small + swap(small, "ctx", 2)

    def whole(value, shape):
        other = swap(value, "tp", 1)
        first = jnp.where(core == 0, value, other)
        second = jnp.where(core == 0, other, value)
        return jnp.concatenate([first, second], axis=0).reshape(shape)

    return (
        whole(later[0][0], prompt_x.shape),
        whole(later[1][0], cont_x.shape),
        whole(dx[0], prompt_x.shape),
        whole(dx[1], cont_x.shape),
        reduced(grad_query, 0),
        reduced(grad_key, 0),
        reduced(grad_value, 0),
        reduced(grad_out, 1),
        reduced(grad_up, 0),
        reduced(grad_down, 1),
        small[:4],
        small[4:],
    )


def solution(mesh):
    placed = (
        P("shard", "ctx", None),
        P(("shard", "ctx"), None, None),
        P(("shard", "ctx")),
        P("shard", "tp"),
        P("shard", "tp"),
        P("shard", "tp"),
        P("tp", "shard"),
        P("shard", "tp"),
        P("tp", "shard"),
        P(None, "shard"),
        P(None, "shard"),
        P("shard", "ctx", None),
        P(("shard", "ctx"), None, None),
    )
    rows = (P("shard", "ctx", None), P(("shard", "ctx"), None, None))
    return jax.shard_map(
        per_device,
        mesh=mesh,
        in_specs=placed,
        out_specs=rows + rows + placed[3:11],
        check_vma=False,
    )
```

time: 903 us -> 486 us (0.54)
  waiting for transfers between devices: 532 us -> 202 us
  Pallas kernels: 0 us -> 113 us
  matrix products: 119 us -> 10.4 us
  other arithmetic: 97.1 us -> 23.1 us
  starting transfers between devices: 1.96 us -> 68 us
  local copies, waits for them, and re-layouts: 74.7 us -> 33.2 us
  blocking collectives: 54.3 us -> 20.7 us
    psum x5 -> x0, waiting for transfers between devices: 388 us -> none  [the longest x4 308 us: over_heads(): return lax.psum(partial_sum, 'tp')]
    ppermute x0 -> x83, waiting for transfers between devices: none -> 202 us  [swap(): return lax.ppermute(value, axis, [(i, i ^ bit) for i in range(size)])]
    pallas_call x0 -> x24, Pallas kernels: none -> 113 us  [call(): pl.pallas_call(kernel, out_shape=shapes, in_specs=[pl.BlockSpec(memory_sp...]
    dot_general x30 -> x6, matrix products: 119 us -> 10.4 us  [tn(): lax.dot_general(left, right, (((0,), (0,)), ((), ())), preferred_element_...]
    reduce_scatter x8 -> x0, waiting for transfers between devices: 105 us -> none  [the longest x1 36.8 us: per_device(): lax.psum_scatter(prompt_val_grad, 'ctx', scatter_dimension=1, tiled=True)]
    ppermute x0 -> x83, starting transfers between devices: none -> 68 us  [swap(): return lax.ppermute(value, axis, [(i, i ^ bit) for i in range(size)])]
    reduce_sum x22 -> x0, other arithmetic: 56.8 us -> none  [the longest x8 21.2 us: layer_norm(): return centred * lax.rsqrt(spread + EPSILON) * norm_gain + norm_bias]
    slice x13 -> x1, local copies, waits for them, and re-layouts: 27.4 us -> 0.61 us  [per_device(): small[4:]]
  transfers between devices with their start and end apart: 19 -> 83, of which waited for: 13 -> 34; matrix products, arithmetic and copies ran while one was open for 12% -> 7% of each run, Pallas kernels for 0% -> 24%
where the time goes in v1:
time: 486 us; the launch traced here: 481 us
  waiting for transfers between devices  202 us (42%)
  Pallas kernels  113 us (23%)
  starting transfers between devices  68 us (14%)
  local copies, waits for them, and re-layouts  33.2 us (7%)
  other arithmetic  23.1 us (5%)
  blocking collectives  20.7 us (4%)
  matrix products  10.4 us (2%)
  between operations  10.3 us (2%)
    ppermute x83, waiting for transfers between devices, swap(): return lax.ppermute(value, axis, [(i, i ^ bit) for i in range(size)])  202 us
    pallas_call x24, Pallas kernels, call(): pl.pallas_call(kernel, out_shape=shapes, in_specs=[pl.BlockSpec(memory_sp...  113 us
    ppermute x83, starting transfers between devices, swap(): return lax.ppermute(value, axis, [(i, i ^ bit) for i in range(size)])  68 us
    unnamed x233, local copies, waits for them, and re-layouts  29.4 us
    all_gather x2, blocking collectives, wide(): full = lax.all_gather(small, 'shard', axis=1, tiled=True)  20.7 us
    dot_general x6, matrix products, tn(): lax.dot_general(left, right, (((0,), (0,)), ((), ())), preferred_element_...  10.4 us
  transfers between devices with their start and end apart: 83, of which 34 were waited for; matrix products, arithmetic and copies ran while one was open for 7% of the time, Pallas kernels for 24%

profile of v1, /device:TPU:0, one launch (start us, length us, event | category | flops | bytes accessed | tf_op | source)
XLA Modules:
  0.0 480.9 jit_solution(12174000608973370068)
XLA Ops:
  1.9 4.1 collective-permute-start.5
  11.2 14.2 %all_gather.6 = bf16[4,1024]{1,0:T(4,128)(2,1)S(1)} all-gather(bf16[4,512]{1,0:T(4,128)(2,1)} %param.49), channel_id=1, replica_groups=mesh['shard'=2,'ctx'=4,'tp'=4] {'shard'}, dimensions={1}, use_global_device_ids=true | all-gather | bytes 12288 | tf_op jit(solution)/shard_map/all_gather | solution.py:537
  25.4 4.0 collective-permute-done.5.xo
  35.1 6.4 %all_gather.7 = bf16[4,1024]{1,0:T(4,128)(2,1)S(1)} all-gather(bf16[4,512]{1,0:T(4,128)(2,1)S(1)} %copy-done.112), channel_id=1, replica_groups=mesh['shard'=2,'ctx'=4,'tp'=4] {'shard'}, dimensions={1}, use_global_device_ids=true | all-gather | bytes 12288 | tf_op jit(solution)/shard_map/all_gather | solution.py:537
  50.9 4.8 qkv_prompt.1
  55.7 4.8 qkv_cont.1
  62.2 5.1 %kv_1.1 = (bf16[512,256]{1,0:T(8,128)(2,1)S(1)}, bf16[512,256]{1,0:T(8,128)(2,1)S(1)}) custom-call(s32[7]{0:T(128)S(1)} %pad_add_fusion.idx.refs_0_, bf16[256,1024]{1,0:T(8,128)(2,1)} %collective-permute-done.3.xo, bf16[256,1024]{1,0:T(8,128)(2,1)} %collective-permute-done.4.xt, f32[1,1024]{1,0:T(1,128)S(1)} %get-tuple-element.263.gain, ...), custom_call_target="tpu_custom_call" | custom-call | flops 536870912 | bytes 4399104 | tf_op jit(solution)/shard_map/kv_1/pallas_call | solution.py:462
  68.3 5.0 %kv_2.1 = (bf16[512,256]{1,0:T(8,128)(2,1)S(1)}, bf16[512,256]{1,0:T(8,128)(2,1)S(1)}) custom-call(s32[7]{0:T(128)S(1)} %pad_add_fusion.idx.refs_0_, bf16[256,1024]{1,0:T(8,128)(2,1)} %collective-permute-done.5.xo, bf16[256,1024]{1,0:T(8,128)(2,1)S(1)} %collective-permute-done.6.xt, f32[1,1024]{1,0:T(1,128)S(1)} %get-tuple-element.263.gain, ...), custom_call_target="tpu_custom_call" | custom-call | flops 536870912 | bytes 4399104 | tf_op jit(solution)/shard_map/kv_2/pallas_call | solution.py:462
  73.3 5.4 %kv_3.1 = (bf16[512,256]{1,0:T(8,128)(2,1)S(1)}, bf16[512,256]{1,0:T(8,128)(2,1)S(1)}) custom-call(s32[7]{0:T(128)S(1)} %pad_add_fusion.idx.refs_0_, bf16[256,1024]{1,0:T(8,128)(2,1)} %collective-permute-done.7.xo, bf16[256,1024]{1,0:T(8,128)(2,1)S(1)} %collective-permute-done.8.xt, f32[1,1024]{1,0:T(1,128)S(1)} %get-tuple-element.263.gain, ...), custom_call_target="tpu_custom_call" | custom-call | flops 536870912 | bytes 4399104 | tf_op jit(solution)/shard_map/kv_3/pallas_call | solution.py:462
  78.8 6.3 %attend_prompt.1 = (bf16[256,256]{1,0:T(8,128)(2,1)S(1)}, bf16[256,256]{1,0:T(8,128)(2,1)S(1)}, bf16[2,4,1024,256]{3,2,1,0:T(8,128)(2,1)S(1)}) custom-call(s32[7]{0:T(128)S(1)} %pad_add_fusion.idx.refs_0_, bf16[512,256]{1,0:T(8,128)(2,1)S(1)} %get-tuple-element.105.q.refs_6_, bf16[512,256]{1,0:T(8,128)(2,1)S(1)} %get-tuple-element.106.k0.refs_7_.refs_10_, ...), custom_call_target="tpu_custom_call" | custom-call | flops 2147483648 | bytes 6815744 | tf_op jit(solution)/shard_map/attend_prompt/pallas_call | solution.py:462
  89.3 6.8 %attend_cont.1 = (bf16[256,256]{1,0:T(8,128)(2,1)S(1)}, bf16[256,256]{1,0:T(8,128)(2,1)S(1)}, bf16[4,2,1024,256]{3,2,1,0:T(8,128)(2,1)S(1)}, bf16[4,2,128,256]{3,2,1,0:T(8,128)(2,1)S(1)}) custom-call(s32[7]{0:T(128)S(1)} %pad_add_fusion.idx.refs_0_, bf16[512,256]{1,0:T(8,128)(2,1)S(1)} %get-tuple-element.121.q.refs_7_, ...), custom_call_target="tpu_custom_call" | custom-call | flops 2147483648 | bytes 7864320 | tf_op jit(solution)/shard_map/attend_cont/pallas_call | solution.py:462
  98.1 5.7 %after_attention.2 = (f32[256,1024]{1,0:T(8,128)S(1)}, f32[256,1024]{1,0:T(8,128)S(1)}, bf16[256,1024]{1,0:T(8,128)(2,1)S(1)}) custom-call(s32[7]{0:T(128)S(1)} %pad_add_fusion.idx.refs_0_, bf16[512,1024]{1,0:T(8,128)(2,1)S(1)} %bitcast.106, bf16[256,256]{1,0:T(8,128)(2,1)S(1)} %get-tuple-element.114.o0, bf16[256,256]{1,0:T(8,128)(2,1)S(1)} %collective-permute-done.9.o1, ...), custom_call_target="tpu_custom_call" | custom-call | flops 536870912 | bytes 6307840 | tf_op jit(solution)/shard_map/after_attention/pallas_call | solution.py:462
  106.8 4.8 collective-permute-done.23.o2
  112.9 5.0 %after_attention.3 = (f32[256,1024]{1,0:T(8,128)S(1)}, f32[256,1024]{1,0:T(8,128)S(1)}, bf16[256,1024]{1,0:T(8,128)(2,1)S(1)}) custom-call(s32[7]{0:T(128)S(1)} %pad_add_fusion.idx.refs_0_, bf16[512,1024]{1,0:T(8,128)(2,1)S(1)} %bitcast.109, bf16[256,256]{1,0:T(8,128)(2,1)S(1)} %get-tuple-element.124.o0, bf16[256,256]{1,0:T(8,128)(2,1)S(1)} %collective-permute-done.22.o1, ...), custom_call_target="tpu_custom_call" | custom-call | flops 536870912 | bytes 6307840 | tf_op jit(solution)/shard_map/after_attention/pallas_call | solution.py:462
  119.4 4.0 up_down.2
  125.5 4.0 up_down.3
  134.3 11.7 %collective-permute-done.20.theirs = bf16[256,1024]{1,0:T(8,128)(2,1)S(1)} collective-permute-done((bf16[256,1024]{1,0:T(8,128)(2,1)S(1)}, bf16[256,1024]{1,0:T(8,128)(2,1)S(1)}, u32[]{:S(2)}, u32[]{:S(2)}) %collective-permute-start.20) | collective-permute-done | bytes 524320 | tf_op jit(solution)/shard_map/ppermute | solution.py:487
  146.0 3.8 last_norm.2
  150.6 5.7 %collective-permute-done.27.theirs = bf16[256,1024]{1,0:T(8,128)(2,1)S(1)} collective-permute-done((bf16[256,1024]{1,0:T(8,128)(2,1)S(1)}, bf16[256,1024]{1,0:T(8,128)(2,1)S(1)}, u32[]{:S(2)}, u32[]{:S(2)}) %collective-permute-start.27) | collective-permute-done | bytes 524320 | tf_op jit(solution)/shard_map/ppermute | solution.py:487
  156.3 4.0 last_norm.3
  175.8 3.8 down_up.2
  180.1 3.6 down_up.3
  183.8 3.8 fusion.30
  198.5 10.3 %collective-permute-done.31.theirs = bf16[256,1024]{1,0:T(8,128)(2,1)S(1)} collective-permute-done((bf16[256,1024]{1,0:T(8,128)(2,1)S(1)}, bf16[256,1024]{1,0:T(8,128)(2,1)S(1)}, u32[]{:S(2)}, u32[]{:S(2)}) %collective-permute-start.31) | collective-permute-done | bytes 524320 | tf_op jit(solution)/shard_map/ppermute | solution.py:487
  208.8 4.0 middle_norms.2
  212.9 6.4 %collective-permute-done.35.theirs = bf16[256,1024]{1,0:T(8,128)(2,1)S(1)} collective-permute-done((bf16[256,1024]{1,0:T(8,128)(2,1)S(1)}, bf16[256,1024]{1,0:T(8,128)(2,1)S(1)}, u32[]{:S(2)}, u32[]{:S(2)}) %collective-permute-start.35) | collective-permute-done | bytes 524320 | tf_op jit(solution)/shard_map/ppermute | solution.py:487
  219.3 4.2 middle_norms.3
  226.7 9.2 %collective-permute-done.69 = bf16[512,1024]{1,0:T(8,128)(2,1)S(1)} collective-permute-done((bf16[512,1024]{1,0:T(8,128)(2,1)S(1)}, bf16[512,1024]{1,0:T(8,128)(2,1)S(1)}, u32[]{:S(2)}, u32[]{:S(2)}) %collective-permute-start.69) | collective-permute-done | bytes 1048608 | tf_op jit(solution)/shard_map/ppermute | solution.py:487
  238.7 10.4 %attend_prompt_back.1 = (bf16[512,256]{1,0:T(8,128)(2,1)S(1)}, f32[512,256]{1,0:T(8,128)S(1)}, f32[512,256]{1,0:T(8,128)S(1)}, f32[512,256]{1,0:T(8,128)S(1)}, f...) custom-call(s32[7]{0:T(128)S(1)} %pad_add_fusion.idx.refs_0_, ...), custom_call_target="tpu_custom_call" | custom-call | flops 4294967296 | bytes 14352384 | tf_op jit(solution)/shard_map/attend_prompt_back/pallas_call | solution.py:462
  253.2 12.5 %attend_cont_back.1 = (bf16[512,256]{1,0:T(8,128)(2,1)S(1)}, bf16[512,256]{1,0:T(8,128)(2,1)S(1)}, bf16[512,256]{1,0:T(8,128)(2,1)S(1)}, bf16[512,256]{1,0:T(8,1...) custom-call(s32[7]{0:T(128)S(1)} %pad_add_fusion.idx.refs_0_, ...), custom_call_target="tpu_custom_call" | custom-call | flops 4294967296 | bytes 18022400 | tf_op jit(solution)/shard_map/attend_cont_back/pallas_call | solution.py:462
  279.0 4.6 collective-permute-done.64
  287.0 3.5 collective-permute-start.76
  290.9 17.9 %collective-permute-done.76 = bf16[256,512]{1,0:T(8,128)(2,1)S(1)} collective-permute-done((bf16[256,512]{1,0:T(8,128)(2,1)S(1)}, bf16[256,512]{1,0:T(8,128)(2,1)S(1)}, u32[]{:S(2)}, u32[]{:S(2)}) %collective-permute-start.76) | collective-permute-done | bytes 262176 | tf_op jit(solution)/shard_map/ppermute | solution.py:487
  308.9 11.2 %collective-permute-done.71 = bf16[128,1024]{1,0:T(8,128)(2,1)S(1)} collective-permute-done((bf16[128,1024]{1,0:T(8,128)(2,1)S(1)}, bf16[128,1024]{1,0:T(8,128)(2,1)S(1)}, u32[]{:S(2)}, u32[]{:S(2)}) %collective-permute-start.71) | collective-permute-done | bytes 262176 | tf_op jit(solution)/shard_map/ppermute | solution.py:487
  320.2 8.2 %collective-permute-done.65 = bf16[2,64,512]{2,1,0:T(8,128)(2,1)S(1)} collective-permute-done((bf16[2,64,512]{2,1,0:T(8,128)(2,1)S(1)}, bf16[2,64,512]{2,1,0:T(8,128)(2,1)S(1)}, u32[]{:S(2)}, u32[]{:S(2)}) %collective-permute-start.65) | collective-permute-done | bytes 131104 | tf_op jit(solution)/shard_map/ppermute | solution.py:487
  328.4 5.4 %collective-permute-done.50 = bf16[2,128,256]{2,1,0:T(8,128)(2,1)S(1)} collective-permute-done((bf16[2,128,256]{2,1,0:T(8,128)(2,1)S(1)}, bf16[2,128,256]{2,1,0:T(8,128)(2,1)S(1)}, u32[]{:S(2)}, u32[]{:S(2)}) %collective-permute-start.50) | collective-permute-done | bytes 131104 | tf_op jit(solution)/shard_map/ppermute | solution.py:487
  335.2 4.2 collective-permute-done.66
  340.4 4.5 collective-permute-done.51
  351.7 18.9 %collective-permute-done.39.k2 = bf16[512,256]{1,0:T(8,128)(2,1)S(1)} collective-permute-done((bf16[512,256]{1,0:T(8,128)(2,1)S(1)}, bf16[512,256]{1,0:T(8,128)(2,1)S(1)}, u32[]{:S(2)}, u32[]{:S(2)}) %collective-permute-start.39) | collective-permute-done | bytes 262176 | tf_op jit(solution)/shard_map/ppermute | solution.py:487
  376.3 6.9 %collective-permute-done.67 = bf16[64,512]{1,0:T(8,128)(2,1)S(1)} collective-permute-done((bf16[64,512]{1,0:T(8,128)(2,1)S(1)}, bf16[64,512]{1,0:T(8,128)(2,1)S(1)}, u32[]{:S(2)}, u32[]{:S(2)}) %collective-permute-start.67) | collective-permute-done | bytes 65568 | tf_op jit(solution)/shard_map/ppermute | solution.py:487
  391.2 3.7 collective-permute-done.53
  401.4 19.8 %collective-permute-done.60 = bf16[2,128,256]{2,1,0:T(8,128)(2,1)S(1)} collective-permute-done((bf16[2,128,256]{2,1,0:T(8,128)(2,1)S(1)}, bf16[2,128,256]{2,1,0:T(8,128)(2,1)S(1)}, u32[]{:S(2)}, u32[]{:S(2)}) %collective-permute-start.60) | collective-permute-done | bytes 131104 | tf_op jit(solution)/shard_map/ppermute | solution.py:487
  421.8 4.9 %collective-permute-done.55 = bf16[2,128,256]{2,1,0:T(8,128)(2,1)S(1)} collective-permute-done((bf16[2,128,256]{2,1,0:T(8,128)(2,1)S(1)}, bf16[2,128,256]{2,1,0:T(8,128)(2,1)S(1)}, u32[]{:S(2)}, u32[]{:S(2)}) %collective-permute-start.55) | collective-permute-done | bytes 131104 | tf_op jit(solution)/shard_map/ppermute | solution.py:487
  427.7 5.4 %collective-permute-done.61 = bf16[128,256]{1,0:T(8,128)(2,1)S(1)} collective-permute-done((bf16[128,256]{1,0:T(8,128)(2,1)S(1)}, bf16[128,256]{1,0:T(8,128)(2,1)S(1)}, u32[]{:S(2)}, u32[]{:S(2)}) %collective-permute-start.61) | collective-permute-done | bytes 65568 | tf_op jit(solution)/shard_map/ppermute | solution.py:487
  433.2 6.5 %collective-permute-done.56 = bf16[128,256]{1,0:T(8,128)(2,1)S(1)} collective-permute-done((bf16[128,256]{1,0:T(8,128)(2,1)S(1)}, bf16[128,256]{1,0:T(8,128)(2,1)S(1)}, u32[]{:S(2)}, u32[]{:S(2)}) %collective-permute-start.56) | collective-permute-done | bytes 65568 | tf_op jit(solution)/shard_map/ppermute | solution.py:487
  457.2 3.2 collective-permute-done.44.theirs
  468.5 3.7 collective-permute-done.81
  473.5 3.3 collective-permute-done.82
  (496 shorter events, 151.3 us)
Async XLA Ops:
  1.9 27.5 %collective-permute-start.5 = (bf16[256,1024]{1,0:T(8,128)(2,1)S(1)}, bf16[256,1024]{1,0:T(8,128)(2,1)}, u32[]{:S(2)}, u32[]{:S(2)}) collective-permute-start(bf16[256,1024]{1,0:T(8,128)(2,1)S(1)} %constant_dynamic-slice_fusion.55), channel_id=1, source_target_pairs={{0,8},{4,12},{8,0},{12,4},{1,9},{5,13},{9,1},{13,5},{2,10},{6,14},... | collective-permute-start | bytes 1572872 | tf_op jit(solution)/shard_map/ppermute | solution.py:487
  6.0 23.9 %collective-permute-start.12 = (bf16[256,512]{1,0:T(8,128)(2,1)}, bf16[256,512]{1,0:T(8,128)(2,1)S(1)}, u32[]{:S(2)}, u32[]{:S(2)}) collective-permute-start(bf16[256,512]{1,0:T(8,128)(2,1)} %refs_3_.3), channel_id=1, source_target_pairs={{0,16},{16,0},{1,17},{17,1},{2,18},{18,2},{3,19},{19,3},{4,20},{20... | collective-permute-start | bytes 786440 | tf_op jit(solution)/shard_map/ppermute | solution.py:487
  7.6 27.5 %collective-permute-start.3 = (bf16[256,1024]{1,0:T(8,128)(2,1)S(1)}, bf16[256,1024]{1,0:T(8,128)(2,1)}, u32[]{:S(2)}, u32[]{:S(2)}) collective-permute-start(bf16[256,1024]{1,0:T(8,128)(2,1)S(1)} %constant_dynamic-slice_fusion.55), channel_id=1, source_target_pairs={{0,4},{4,0},{8,12},{12,8},{1,5},{5,1},{9,13},{13,9},{2,6},{6,2},{1... | collective-permute-start | bytes 1572872 | tf_op jit(solution)/shard_map/ppermute | solution.py:487
  9.1 24.3 %collective-permute-start.1 = (bf16[512,256]{1,0:T(8,128)(2,1)}, bf16[512,256]{1,0:T(8,128)(2,1)S(1)}, u32[]{:S(2)}, u32[]{:S(2)}) collective-permute-start(bf16[512,256]{1,0:T(8,128)(2,1)} %wka.13), channel_id=1, source_target_pairs={{0,16},{16,0},{1,17},{17,1},{2,18},{18,2},{3,19},{19,3},{4,20},{20... | collective-permute-start | bytes 786440 | tf_op jit(solution)/shard_map/ppermute | solution.py:487
  9.6 31.9 %collective-permute-start.2 = (bf16[512,256]{1,0:T(8,128)(2,1)}, bf16[512,256]{1,0:T(8,128)(2,1)S(1)}, u32[]{:S(2)}, u32[]{:S(2)}) collective-permute-start(bf16[512,256]{1,0:T(8,128)(2,1)} %wva.13), channel_id=1, source_target_pairs={{0,16},{16,0},{1,17},{17,1},{2,18},{18,2},{3,19},{19,3},{4,20},{20... | collective-permute-start | bytes 786440 | tf_op jit(solution)/shard_map/ppermute | solution.py:487
  35.0 25.6 %collective-permute-start.4 = (bf16[256,1024]{1,0:T(8,128)(2,1)}, bf16[256,1024]{1,0:T(8,128)(2,1)}, u32[]{:S(2)}, u32[]{:S(2)}) collective-permute-start(bf16[256,1024]{1,0:T(8,128)(2,1)} %collective-permute-done.3.xo), channel_id=1, source_target_pairs={{0,1},{1,0},{2,3},{3,2},{4,5},{5,4},{6,7},{7,6},{8,9},{9,8},{10,11... | collective-permute-start | bytes 1572872 | tf_op jit(solution)/shard_map/ppermute | solution.py:487
  42.3 25.0 %collective-permute-start.6 = (bf16[256,1024]{1,0:T(8,128)(2,1)}, bf16[256,1024]{1,0:T(8,128)(2,1)S(1)}, u32[]{:S(2)}, u32[]{:S(2)}) collective-permute-start(bf16[256,1024]{1,0:T(8,128)(2,1)} %collective-permute-done.5.xo), channel_id=1, source_target_pairs={{0,1},{1,0},{2,3},{3,2},{4,5},{5,4},{6,7},{7,6},{8,9},{9,8},{10,11... | collective-permute-start | bytes 1572872 | tf_op jit(solution)/shard_map/ppermute | solution.py:487
  42.8 30.5 %collective-permute-start.8 = (bf16[256,1024]{1,0:T(8,128)(2,1)}, bf16[256,1024]{1,0:T(8,128)(2,1)S(1)}, u32[]{:S(2)}, u32[]{:S(2)}) collective-permute-start(bf16[256,1024]{1,0:T(8,128)(2,1)} %collective-permute-done.7.xo), channel_id=1, source_target_pairs={{0,1},{1,0},{2,3},{3,2},{4,5},{5,4},{6,7},{7,6},{8,9},{9,8},{10,11... | collective-permute-start | bytes 1572872 | tf_op jit(solution)/shard_map/ppermute | solution.py:487
  43.6 44.9 %collective-permute-start.13 = (bf16[2,256,512]{2,1,0:T(8,128)(2,1)}, bf16[2,256,512]{2,1,0:T(8,128)(2,1)S(1)}, u32[]{:S(2)}, u32[]{:S(2)}) collective-permute-start(bf16[2,256,512]{2,1,0:T(8,128)(2,1)} %pad_maximum_fusion.8.w0), channel_id=1, source_target_pairs={{0,1},{1,0},{2,3},{3,2},{4,5},{5,4},{6,7},{7,6},{8,9},{9,8},{10,11... | collective-permute-start | bytes 1572872 | tf_op jit(solution)/shard_map/ppermute | solution.py:487
  45.7 43.0 %collective-permute-start.15 = (bf16[2,256,512]{2,1,0:T(8,128)(2,1)}, bf16[2,256,512]{2,1,0:T(8,128)(2,1)S(1)}, u32[]{:S(2)}, u32[]{:S(2)}) collective-permute-start(bf16[2,256,512]{2,1,0:T(8,128)(2,1)} %collective-permute-done.14.w2), channel_id=1, source_target_pairs={{0,1},{1,0},{2,3},{3,2},{4,5},{5,4},{6,7},{7,6},{8,9},{9,8},{10,11... | collective-permute-start | bytes 1572872 | tf_op jit(solution)/shard_map/ppermute | solution.py:487
  60.6 58.8 %collective-permute-start.17 = (bf16[512,1024]{1,0:T(8,128)(2,1)S(1)}, bf16[512,1024]{1,0:T(8,128)(2,1)S(1)}, u32[]{:S(2)}, u32[]{:S(2)}) collective-permute-start(bf16[512,1024]{1,0:T(8,128)(2,1)S(1)} %copy-done.42), channel_id=1, source_target_pairs={{0,16},{16,0},{1,17},{17,1},{2,18},{18,2},{3,19},{19,3},{4,20},{20... | collective-permute-start | bytes 3145736 | tf_op jit(solution)/shard_map/ppermute | solution.py:487
  67.3 52.1 %collective-permute-start.18 = (bf16[1024,512]{1,0:T(8,128)(2,1)S(1)}, bf16[1024,512]{1,0:T(8,128)(2,1)S(1)}, u32[]{:S(2)}, u32[]{:S(2)}) collective-permute-start(bf16[1024,512]{1,0:T(8,128)(2,1)S(1)} %copy-done.44), channel_id=1, source_target_pairs={{0,16},{16,0},{1,17},{17,1},{2,18},{18,2},{3,19},{19,3},{4,20},{20... | collective-permute-start | bytes 3145736 | tf_op jit(solution)/shard_map/ppermute | solution.py:487
  104.9 14.5 %collective-permute-start.16 = (bf16[256,1024]{1,0:T(8,128)(2,1)S(1)}, bf16[256,1024]{1,0:T(8,128)(2,1)S(1)}, u32[]{:S(2)}, u32[]{:S(2)}) collective-permute-start(bf16[256,1024]{1,0:T(8,128)(2,1)S(1)} %get-tuple-element.116.n3o), channel_id=1, source_target_pairs={{0,1},{1,0},{2,3},{3,2},{4,5},{5,4},{6,7},{7,6},{8,9},{9,8},{10,11... | collective-permute-start | bytes 1572872 | tf_op jit(solution)/shard_map/ppermute | solution.py:487
  131.1 14.8 %collective-permute-start.20 = (bf16[256,1024]{1,0:T(8,128)(2,1)S(1)}, bf16[256,1024]{1,0:T(8,128)(2,1)S(1)}, u32[]{:S(2)}, u32[]{:S(2)}) collective-permute-start(bf16[256,1024]{1,0:T(8,128)(2,1)S(1)} %add_convert_fusion.7.mine), channel_id=1, source_target_pairs={{0,2},{1,3},{2,0},{3,1},{4,6},{5,7},{6,4},{7,5},{8,10},{9,11},{10,... | collective-permute-start | bytes 1572872 | tf_op jit(solution)/shard_map/ppermute | solution.py:487
  132.9 23.4 %collective-permute-start.27 = (bf16[256,1024]{1,0:T(8,128)(2,1)S(1)}, bf16[256,1024]{1,0:T(8,128)(2,1)S(1)}, u32[]{:S(2)}, u32[]{:S(2)}) collective-permute-start(bf16[256,1024]{1,0:T(8,128)(2,1)S(1)} %add_convert_fusion.6.mine), channel_id=1, source_target_pairs={{0,2},{1,3},{2,0},{3,1},{4,6},{5,7},{6,4},{7,5},{8,10},{9,11},{10,... | collective-permute-start | bytes 1572872 | tf_op jit(solution)/shard_map/ppermute | solution.py:487
  150.6 20.9 %collective-permute-start.29 = (bf16[256,1024]{1,0:T(8,128)(2,1)}, bf16[256,1024]{1,0:T(8,128)(2,1)}, u32[]{:S(2)}, u32[]{:S(2)}) collective-permute-start(bf16[256,1024]{1,0:T(8,128)(2,1)} %get-tuple-element.131.dmo), channel_id=1, source_target_pairs={{0,1},{1,0},{2,3},{3,2},{4,5},{5,4},{6,7},{7,6},{8,9},{9,8},{10,11... | collective-permute-start | bytes 1572872 | tf_op jit(solution)/shard_map/ppermute | solution.py:487
  161.0 19.0 %collective-permute-start.33 = (bf16[256,1024]{1,0:T(8,128)(2,1)}, bf16[256,1024]{1,0:T(8,128)(2,1)S(1)}, u32[]{:S(2)}, u32[]{:S(2)}) collective-permute-start(bf16[256,1024]{1,0:T(8,128)(2,1)} %get-tuple-element.139.dmo), channel_id=1, source_target_pairs={{0,1},{1,0},{2,3},{3,2},{4,5},{5,4},{6,7},{7,6},{8,9},{9,8},{10,11... | collective-permute-start | bytes 1572872 | tf_op jit(solution)/shard_map/ppermute | solution.py:487
  170.8 21.7 %collective-permute-start.28 = (bf16[256,1024]{1,0:T(8,128)(2,1)S(1)}, bf16[256,1024]{1,0:T(8,128)(2,1)S(1)}, u32[]{:S(2)}, u32[]{:S(2)}) collective-permute-start(bf16[256,1024]{1,0:T(8,128)(2,1)S(1)} %copy-done.38), channel_id=1, source_target_pairs={{0,1},{1,0},{2,3},{3,2},{4,5},{5,4},{6,7},{7,6},{8,9},{9,8},{10,11... | collective-permute-start | bytes 1572872 | tf_op jit(solution)/shard_map/ppermute | solution.py:487
  171.3 26.0 %collective-permute-start.21 = (bf16[256,1024]{1,0:T(8,128)(2,1)S(1)}, bf16[256,1024]{1,0:T(8,128)(2,1)S(1)}, u32[]{:S(2)}, u32[]{:S(2)}) collective-permute-start(bf16[256,1024]{1,0:T(8,128)(2,1)S(1)} %copy-done.36), channel_id=1, source_target_pairs={{0,1},{1,0},{2,3},{3,2},{4,5},{5,4},{6,7},{7,6},{8,9},{9,8},{10,11... | collective-permute-start | bytes 1572872 | tf_op jit(solution)/shard_map/ppermute | solution.py:487
  179.5 14.3 %collective-permute-start.30 = (bf16[256,1024]{1,0:T(8,128)(2,1)S(1)}, bf16[256,1024]{1,0:T(8,128)(2,1)S(1)}, u32[]{:S(2)}, u32[]{:S(2)}) collective-permute-start(bf16[256,1024]{1,0:T(8,128)(2,1)S(1)} %get-tuple-element.134), channel_id=1, source_target_pairs={{0,1},{1,0},{2,3},{3,2},{4,5},{5,4},{6,7},{7,6},{8,9},{9,8},{10,11... | collective-permute-start | bytes 1572872 | tf_op jit(solution)/shard_map/ppermute | solution.py:487
  187.8 35.8 %collective-permute-start.74 = (bf16[1024,512]{1,0:T(8,128)(2,1)S(1)}, bf16[1024,512]{1,0:T(8,128)(2,1)}, u32[]{:S(2)}, u32[]{:S(2)}) collective-permute-start(bf16[1024,512]{1,0:T(8,128)(2,1)S(1)} %constant_dynamic-slice_fusion.35), channel_id=1, source_target_pairs={{0,16},{16,0},{1,17},{17,1},{2,18},{18,2},{3,19},{19,3},{4,20},{20... | collective-permute-start | bytes 3145736 | tf_op jit(solution)/shard_map/ppermute | solution.py:487
  192.5 43.4 %collective-permute-start.69 = (bf16[512,1024]{1,0:T(8,128)(2,1)S(1)}, bf16[512,1024]{1,0:T(8,128)(2,1)S(1)}, u32[]{:S(2)}, u32[]{:S(2)}) collective-permute-start(bf16[512,1024]{1,0:T(8,128)(2,1)S(1)} %constant_dynamic-slice_fusion.8), channel_id=1, source_target_pairs={{0,16},{16,0},{1,17},{17,1},{2,18},{18,2},{3,19},{19,3},{4,20},{20... | collective-permute-start | bytes 3145736 | tf_op jit(solution)/shard_map/ppermute | solution.py:487
  194.0 14.8 %collective-permute-start.31 = (bf16[256,1024]{1,0:T(8,128)(2,1)S(1)}, bf16[256,1024]{1,0:T(8,128)(2,1)S(1)}, u32[]{:S(2)}, u32[]{:S(2)}) collective-permute-start(bf16[256,1024]{1,0:T(8,128)(2,1)S(1)} %add_convert_fusion.5.mine), channel_id=1, source_target_pairs={{0,2},{1,3},{2,0},{3,1},{4,6},{5,7},{6,4},{7,5},{8,10},{9,11},{10,... | collective-permute-start | bytes 1572872 | tf_op jit(solution)/shard_map/ppermute | solution.py:487
  195.7 23.6 %collective-permute-start.35 = (bf16[256,1024]{1,0:T(8,128)(2,1)S(1)}, bf16[256,1024]{1,0:T(8,128)(2,1)S(1)}, u32[]{:S(2)}, u32[]{:S(2)}) collective-permute-start(bf16[256,1024]{1,0:T(8,128)(2,1)S(1)} %add_convert_fusion.4.mine), channel_id=1, source_target_pairs={{0,2},{1,3},{2,0},{3,1},{4,6},{5,7},{6,4},{7,5},{8,10},{9,11},{10,... | collective-permute-start | bytes 1572872 | tf_op jit(solution)/shard_map/ppermute | solution.py:487
  212.8 25.0 %collective-permute-start.32 = (bf16[256,1024]{1,0:T(8,128)(2,1)S(1)}, bf16[256,1024]{1,0:T(8,128)(2,1)S(1)}, u32[]{:S(2)}, u32[]{:S(2)}) collective-permute-start(bf16[256,1024]{1,0:T(8,128)(2,1)S(1)} %get-tuple-element.136.refs_1_), channel_id=1, source_target_pairs={{0,1},{1,0},{2,3},{3,2},{4,5},{5,4},{6,7},{7,6},{8,9},{9,8},{10,11... | collective-permute-start | bytes 1572872 | tf_op jit(solution)/shard_map/ppermute | solution.py:487
  223.5 29.7 %collective-permute-start.36 = (bf16[256,1024]{1,0:T(8,128)(2,1)S(1)}, bf16[256,1024]{1,0:T(8,128)(2,1)}, u32[]{:S(2)}, u32[]{:S(2)}) collective-permute-start(bf16[256,1024]{1,0:T(8,128)(2,1)S(1)} %get-tuple-element.144.refs_1_), channel_id=1, source_target_pairs={{0,1},{1,0},{2,3},{3,2},{4,5},{5,4},{6,7},{7,6},{8,9},{9,8},{10,11... | collective-permute-start | bytes 1572872 | tf_op jit(solution)/shard_map/ppermute | solution.py:487
  226.3 48.1 %collective-permute-start.75 = (bf16[2,256,512]{2,1,0:T(8,128)(2,1)}, bf16[2,256,512]{2,1,0:T(8,128)(2,1)}, u32[]{:S(2)}, u32[]{:S(2)}) collective-permute-start(bf16[2,256,512]{2,1,0:T(8,128)(2,1)} %pad_maximum_fusion.11), channel_id=1, source_target_pairs={{0,4},{4,0},{8,12},{12,8},{1,5},{5,1},{9,13},{13,9},{2,6},{6,2},{1... | collective-permute-start | bytes 1572872 | tf_op jit(solution)/shard_map/ppermute | solution.py:487
  237.3 39.5 %collective-permute-start.70 = (bf16[2,128,1024]{2,1,0:T(8,128)(2,1)}, bf16[2,128,1024]{2,1,0:T(8,128)(2,1)}, u32[]{:S(2)}, u32[]{:S(2)}) collective-permute-start(bf16[2,128,1024]{2,1,0:T(8,128)(2,1)} %pad_maximum_fusion.9), channel_id=1, source_target_pairs={{0,4},{4,0},{8,12},{12,8},{1,5},{5,1},{9,13},{13,9},{2,6},{6,2},{1... | collective-permute-start | bytes 1572872 | tf_op jit(solution)/shard_map/ppermute | solution.py:487
  265.7 21.3 %collective-permute-start.41 = (bf16[512,256]{1,0:T(8,128)(2,1)S(1)}, bf16[512,256]{1,0:T(8,128)(2,1)S(1)}, u32[]{:S(2)}, u32[]{:S(2)}) collective-permute-start(bf16[512,256]{1,0:T(8,128)(2,1)S(1)} %get-tuple-element.162), channel_id=1, source_target_pairs={{0,4},{4,0},{8,12},{12,8},{1,5},{5,1},{9,13},{13,9},{2,6},{6,2},{1... | collective-permute-start | bytes 786440 | tf_op jit(solution)/shard_map/ppermute | solution.py:487
  267.3 23.3 %collective-permute-start.38 = (bf16[512,256]{1,0:T(8,128)(2,1)S(1)}, bf16[512,256]{1,0:T(8,128)(2,1)S(1)}, u32[]{:S(2)}, u32[]{:S(2)}) collective-permute-start(bf16[512,256]{1,0:T(8,128)(2,1)S(1)} %get-tuple-element.158), channel_id=1, source_target_pairs={{0,4},{4,0},{8,12},{12,8},{1,5},{5,1},{9,13},{13,9},{2,6},{6,2},{1... | collective-permute-start | bytes 786440 | tf_op jit(solution)/shard_map/ppermute | solution.py:487
  267.8 80.3 %collective-permute-start.37 = (bf16[512,256]{1,0:T(8,128)(2,1)S(1)}, bf16[512,256]{1,0:T(8,128)(2,1)S(1)}, u32[]{:S(2)}, u32[]{:S(2)}) collective-permute-start(bf16[512,256]{1,0:T(8,128)(2,1)S(1)} %get-tuple-element.156), channel_id=1, source_target_pairs={{0,4},{4,0},{8,12},{12,8},{1,5},{5,1},{9,13},{13,9},{2,6},{6,2},{1... | collective-permute-start | bytes 786440 | tf_op jit(solution)/shard_map/ppermute | solution.py:487
  283.6 65.1 %collective-permute-start.40 = (bf16[512,256]{1,0:T(8,128)(2,1)S(1)}, bf16[512,256]{1,0:T(8,128)(2,1)S(1)}, u32[]{:S(2)}, u32[]{:S(2)}) collective-permute-start(bf16[512,256]{1,0:T(8,128)(2,1)S(1)} %get-tuple-element.160), channel_id=1, source_target_pairs={{0,4},{4,0},{8,12},{12,8},{1,5},{5,1},{9,13},{13,9},{2,6},{6,2},{1... | collective-permute-start | bytes 786440 | tf_op jit(solution)/shard_map/ppermute | solution.py:487
  286.9 58.7 %collective-permute-start.46 = (bf16[256,1024]{1,0:T(8,128)(2,1)S(1)}, bf16[256,1024]{1,0:T(8,128)(2,1)S(1)}, u32[]{:S(2)}, u32[]{:S(2)}) collective-permute-start(bf16[256,1024]{1,0:T(8,128)(2,1)S(1)} %get-tuple-element.173), channel_id=1, source_target_pairs={{0,1},{1,0},{2,3},{3,2},{4,5},{5,4},{6,7},{7,6},{8,9},{9,8},{10,11... | collective-permute-start | bytes 1572872 | tf_op jit(solution)/shard_map/ppermute | solution.py:487
  287.0 21.8 %collective-permute-start.76 = (bf16[256,512]{1,0:T(8,128)(2,1)S(1)}, bf16[256,512]{1,0:T(8,128)(2,1)S(1)}, u32[]{:S(2)}, u32[]{:S(2)}) collective-permute-start(bf16[256,512]{1,0:T(8,128)(2,1)S(1)} %fusion.64), channel_id=1, source_target_pairs={{0,8},{4,12},{8,0},{12,4},{1,9},{5,13},{9,1},{13,5},{2,10},{6,14},... | collective-permute-start | bytes 786440 | tf_op jit(solution)/shard_map/ppermute | solution.py:487
  290.6 29.4 %collective-permute-start.71 = (bf16[128,1024]{1,0:T(8,128)(2,1)S(1)}, bf16[128,1024]{1,0:T(8,128)(2,1)S(1)}, u32[]{:S(2)}, u32[]{:S(2)}) collective-permute-start(bf16[128,1024]{1,0:T(8,128)(2,1)S(1)} %fusion.63), channel_id=1, source_target_pairs={{0,8},{4,12},{8,0},{12,4},{1,9},{5,13},{9,1},{13,5},{2,10},{6,14},... | collective-permute-start | bytes 786440 | tf_op jit(solution)/shard_map/ppermute | solution.py:487
  308.8 42.3 %collective-permute-start.42 = (bf16[512,256]{1,0:T(8,128)(2,1)S(1)}, bf16[512,256]{1,0:T(8,128)(2,1)S(1)}, u32[]{:S(2)}, u32[]{:S(2)}) collective-permute-start(bf16[512,256]{1,0:T(8,128)(2,1)S(1)} %add_convert_fusion.12), channel_id=1, source_target_pairs={{0,8},{4,12},{8,0},{12,4},{1,9},{5,13},{9,1},{13,5},{2,10},{6,14},... | collective-permute-start | bytes 786440 | tf_op jit(solution)/shard_map/ppermute | solution.py:487
  344.9 25.7 %collective-permute-start.39 = (bf16[512,256]{1,0:T(8,128)(2,1)S(1)}, bf16[512,256]{1,0:T(8,128)(2,1)S(1)}, u32[]{:S(2)}, u32[]{:S(2)}) collective-permute-start(bf16[512,256]{1,0:T(8,128)(2,1)S(1)} %add_convert_fusion.13), channel_id=1, source_target_pairs={{0,8},{4,12},{8,0},{12,4},{1,9},{5,13},{9,1},{13,5},{2,10},{6,14},... | collective-permute-start | bytes 786440 | tf_op jit(solution)/shard_map/ppermute | solution.py:487
  345.6 39.1 %collective-permute-start.77 = (bf16[256,512]{1,0:T(8,128)(2,1)S(1)}, bf16[256,512]{1,0:T(8,128)(2,1)S(1)}, u32[]{:S(2)}, u32[]{:S(2)}) collective-permute-start(bf16[256,512]{1,0:T(8,128)(2,1)S(1)} %fusion.44), channel_id=1, source_target_pairs={{0,8},{4,12},{8,0},{12,4},{1,9},{5,13},{9,1},{13,5},{2,10},{6,14},... | collective-permute-start | bytes 786440 | tf_op jit(solution)/shard_map/ppermute | solution.py:487
  348.1 37.9 %collective-permute-start.72 = (bf16[128,1024]{1,0:T(8,128)(2,1)S(1)}, bf16[128,1024]{1,0:T(8,128)(2,1)S(1)}, u32[]{:S(2)}, u32[]{:S(2)}) collective-permute-start(bf16[128,1024]{1,0:T(8,128)(2,1)S(1)} %fusion.46), channel_id=1, source_target_pairs={{0,8},{4,12},{8,0},{12,4},{1,9},{5,13},{9,1},{13,5},{2,10},{6,14},... | collective-permute-start | bytes 786440 | tf_op jit(solution)/shard_map/ppermute | solution.py:487
  348.8 34.5 %collective-permute-start.67 = (bf16[64,512]{1,0:T(8,128)(2,1)S(1)}, bf16[64,512]{1,0:T(8,128)(2,1)S(1)}, u32[]{:S(2)}, u32[]{:S(2)}) collective-permute-start(bf16[64,512]{1,0:T(8,128)(2,1)S(1)} %fusion.66), channel_id=1, source_target_pairs={{0,8},{4,12},{8,0},{12,4},{1,9},{5,13},{9,1},{13,5},{2,10},{6,14},... | collective-permute-start | bytes 196616 | tf_op jit(solution)/shard_map/ppermute | solution.py:487
  351.1 33.5 %collective-permute-start.52 = (bf16[128,256]{1,0:T(8,128)(2,1)S(1)}, bf16[128,256]{1,0:T(8,128)(2,1)S(1)}, u32[]{:S(2)}, u32[]{:S(2)}) collective-permute-start(bf16[128,256]{1,0:T(8,128)(2,1)S(1)} %fusion.72), channel_id=1, source_target_pairs={{0,8},{4,12},{8,0},{12,4},{1,9},{5,13},{9,1},{13,5},{2,10},{6,14},... | collective-permute-start | bytes 196616 | tf_op jit(solution)/shard_map/ppermute | solution.py:487
  370.6 69.1 %collective-permute-start.47 = (bf16[256,1024]{1,0:T(8,128)(2,1)S(1)}, bf16[256,1024]{1,0:T(8,128)(2,1)S(1)}, u32[]{:S(2)}, u32[]{:S(2)}) collective-permute-start(bf16[256,1024]{1,0:T(8,128)(2,1)S(1)} %add_convert_fusion.2.mine), channel_id=1, source_target_pairs={{0,2},{1,3},{2,0},{3,1},{4,6},{5,7},{6,4},{7,5},{8,10},{9,11},{10,... | collective-permute-start | bytes 1572872 | tf_op jit(solution)/shard_map/ppermute | solution.py:487
  383.2 62.5 %collective-permute-start.43 = (bf16[256,1024]{1,0:T(8,128)(2,1)S(1)}, bf16[256,1024]{1,0:T(8,128)(2,1)S(1)}, u32[]{:S(2)}, u32[]{:S(2)}) collective-permute-start(bf16[256,1024]{1,0:T(8,128)(2,1)S(1)} %get-tuple-element.166), channel_id=1, source_target_pairs={{0,1},{1,0},{2,3},{3,2},{4,5},{5,4},{6,7},{7,6},{8,9},{9,8},{10,11... | collective-permute-start | bytes 1572872 | tf_op jit(solution)/shard_map/ppermute | solution.py:487
  394.9 51.0 %collective-permute-start.78 = (bf16[2,256,512]{2,1,0:T(8,128)(2,1)S(1)}, bf16[2,256,512]{2,1,0:T(8,128)(2,1)S(1)}, u32[]{:S(2)}, u32[]{:S(2)}) collective-permute-start(bf16[2,256,512]{2,1,0:T(8,128)(2,1)S(1)} %pad_maximum_fusion.12), channel_id=1, source_target_pairs={{0,4},{4,0},{8,12},{12,8},{1,5},{5,1},{9,13},{13,9},{2,6},{6,2},{1... | collective-permute-start | bytes 1572872 | tf_op jit(solution)/shard_map/ppermute | solution.py:487
  395.4 54.2 %collective-permute-start.73 = (bf16[2,128,1024]{2,1,0:T(8,128)(2,1)S(1)}, bf16[2,128,1024]{2,1,0:T(8,128)(2,1)S(1)}, u32[]{:S(2)}, u32[]{:S(2)}) collective-permute-start(bf16[2,128,1024]{2,1,0:T(8,128)(2,1)S(1)} %pad_maximum_fusion.10), channel_id=1, source_target_pairs={{0,4},{4,0},{8,12},{12,8},{1,5},{5,1},{9,13},{13,9},{2,6},{6,2},{1... | collective-permute-start | bytes 1572872 | tf_op jit(solution)/shard_map/ppermute | solution.py:487
  398.7 22.4 %collective-permute-start.60 = (bf16[2,128,256]{2,1,0:T(8,128)(2,1)S(1)}, bf16[2,128,256]{2,1,0:T(8,128)(2,1)S(1)}, u32[]{:S(2)}, u32[]{:S(2)}) collective-permute-start(bf16[2,128,256]{2,1,0:T(8,128)(2,1)S(1)} %pad_maximum_fusion.25), channel_id=1, source_target_pairs={{0,4},{4,0},{8,12},{12,8},{1,5},{5,1},{9,13},{13,9},{2,6},{6,2},{1... | collective-permute-start | bytes 393224 | tf_op jit(solution)/shard_map/ppermute | solution.py:487
  445.7 31.7 %collective-permute-start.48 = (bf16[256,1024]{1,0:T(8,128)(2,1)S(1)}, bf16[256,1024]{1,0:T(8,128)(2,1)}, u32[]{:S(2)}, u32[]{:S(2)}) collective-permute-start(bf16[256,1024]{1,0:T(8,128)(2,1)S(1)} %get-tuple-element.175), channel_id=1, source_target_pairs={{0,1},{1,0},{2,3},{3,2},{4,5},{5,4},{6,7},{7,6},{8,9},{9,8},{10,11... | collective-permute-start | bytes 1572872 | tf_op jit(solution)/shard_map/ppermute | solution.py:487
  446.0 14.4 %collective-permute-start.44 = (bf16[256,1024]{1,0:T(8,128)(2,1)S(1)}, bf16[256,1024]{1,0:T(8,128)(2,1)S(1)}, u32[]{:S(2)}, u32[]{:S(2)}) collective-permute-start(bf16[256,1024]{1,0:T(8,128)(2,1)S(1)} %add_convert_fusion.3.mine), channel_id=1, source_target_pairs={{0,2},{1,3},{2,0},{3,1},{4,6},{5,7},{6,4},{7,5},{8,10},{9,11},{10,... | collective-permute-start | bytes 1572872 | tf_op jit(solution)/shard_map/ppermute | solution.py:487
  (151 other events, 1482.5 us)
